TPU v7x, 128 devices: a whole 4x4x4 slice. The times are simulated.
128 devices in a mesh: dp: 16 (over y, z), row: 4 (over x_lo, core), col: 2 (over x_hi).
Axes of the slice: x: 4 (x_hi: 2, x_lo: 2; x = x_hi * 2 + x_lo), y: 4, z: 4, core: 2. Of those that a mesh axis runs over, the one named last changes fastest.
Arguments:
- block_input: bfloat16 [16384, 2048], P(('dp', 'col'), 'row'), may hold values from -6.2 to 6.2
- cotangent: bfloat16 [16384, 2048], P(('dp', 'col'), 'row'), may hold values from -6 to 6
- norm_gains: float32 [2, 2048], P(None, 'row'), may hold values from 0.2 to 2
- gains_first: float32 [2, 2048], P(None, 'row'), may hold values from -56 to 56
- gains_second: float32 [2, 2048], P(None, 'row'), may hold values from 180.224 to 2949.12
- heads_projection_weight: float32 [2048, 2560], P(('row', 'dp'), 'col'), may hold values from -0.125 to 0.125
- heads_first_moment: float32 [2048, 2560], P(('row', 'dp'), 'col'), may hold values from -64 to 64
- heads_second_moment: float32 [2048, 2560], P(('row', 'dp'), 'col'), may hold values from 212.992 to 3440.64
- merge_weight: float32 [2048, 2048], P(('col', 'dp'), 'row'), may hold values from -2 to 2
- merge_first: float32 [2048, 2048], P(('col', 'dp'), 'row'), may hold values from -6 to 6
- merge_second: float32 [2048, 2048], P(('col', 'dp'), 'row'), may hold values from 2.08 to 32
- gating_weight: float32 [2048, 2, 5632], P(('row', 'dp'), None, 'col'), may hold values from -0.125 to 0.125
- gating_first: float32 [2048, 2, 5632], P(('row', 'dp'), None, 'col'), may hold values from -32 to 32
- gating_second: float32 [2048, 2, 5632], P(('row', 'dp'), None, 'col'), may hold values from 52.4288 to 851.968
- down_weight: float32 [5632, 2048], P(('col', 'dp'), 'row'), may hold values from -0.078125 to 0.078125
- down_first: float32 [5632, 2048], P(('col', 'dp'), 'row'), may hold values from -48 to 48
- down_second: float32 [5632, 2048], P(('col', 'dp'), 'row'), may hold values from 155.648 to 2457.6
Outputs:
- block_output: bfloat16 [16384, 2048], P(('dp', 'col'), 'row')
- input_grad: float32 [16384, 2048], P(('dp', 'col'), 'row')
- gains_grad: float32 [2, 2048], P(None, 'row')
- gains_next: float32 [2, 2048], P(None, 'row')
- gains_mean: float32 [2, 2048], P(None, 'row')
- gains_square: float32 [2, 2048], P(None, 'row')
- heads_grad: float32 [2048, 2560], P(('row', 'dp'), 'col')
- heads_next: float32 [2048, 2560], P(('row', 'dp'), 'col')
- heads_mean: float32 [2048, 2560], P(('row', 'dp'), 'col')
- heads_square: float32 [2048, 2560], P(('row', 'dp'), 'col')
- merge_grad: float32 [2048, 2048], P(('col', 'dp'), 'row')
- merge_next: float32 [2048, 2048], P(('col', 'dp'), 'row')
- merge_mean: float32 [2048, 2048], P(('col', 'dp'), 'row')
- merge_square: float32 [2048, 2048], P(('col', 'dp'), 'row')
- gating_grad: float32 [2048, 2, 5632], P(('row', 'dp'), None, 'col')
- gating_next: float32 [2048, 2, 5632], P(('row', 'dp'), None, 'col')
- gating_mean: float32 [2048, 2, 5632], P(('row', 'dp'), None, 'col')
- gating_square: float32 [2048, 2, 5632], P(('row', 'dp'), None, 'col')
- down_grad: float32 [5632, 2048], P(('col', 'dp'), 'row')
- down_next: float32 [5632, 2048], P(('col', 'dp'), 'row')
- down_mean: float32 [5632, 2048], P(('col', 'dp'), 'row')
- down_square: float32 [5632, 2048], P(('col', 'dp'), 'row')
All inputs are finite; a program needn't handle non-finite values.
Results may differ from a plain program's by a relative error of at most 0.025.
Values may be sent and summed in bfloat16 or wider, within the bound.
A program may use at most 192 MiB of HBM per device.

v0:
```python
import jax
import jax.numpy as jnp
from jax import lax
from jax.sharding import PartitionSpec as P

MODEL_WIDTH = 2048
KEY_VALUE_HEADS = 4
HEAD_SIZE = 64
QUERY_PER_GROUP = 8
STEP = 10


EPS_NORM = 1e-05
BETA_ONE = 0.9
BETA_TWO = 0.95
EPS_ADAM = 1e-08
RATE_MATRIX = 0.05
RATE_MERGE = 0.5
RATE_GAIN = 1.0
WEIGHT_DECAY = 0.1
ROPE_BASE = 10000.0
MASK_FILL = -1e30


def rope_tables(positions):
    half_width = HEAD_SIZE // 2
    frequency = ROPE_BASE ** (-jnp.arange(half_width, dtype=jnp.float32) * 2.0 / HEAD_SIZE)
    angles = positions.astype(jnp.float32)[:, None] * frequency[None, :]
    return (jnp.cos(angles), jnp.sin(angles))


def rotate(vector, cosine_rows, sine_rows):
    piece_one, piece_two = jnp.split(vector, 2, axis=-1)
    return jnp.concatenate(
        [
            piece_one * cosine_rows - piece_two * sine_rows,
            piece_two * cosine_rows + piece_one * sine_rows,
        ],
        axis=-1,
    )


def feature_sum(values):
    return lax.psum(values, "row")


def gather_col(values):
    return lax.all_gather(values, "col", axis=0, tiled=True)


def gather_row(values):
    return lax.all_gather(values, "row", axis=0, tiled=True)


def sum_row(left_rows, product, out_rows):

    def partial_value(row_start, row_count):
        return product(left_rows)

    return lax.psum_scatter(
        partial_value(jnp.int32(0), out_rows * lax.axis_size("row")),
        "row",
        scatter_dimension=0,
        tiled=True,
    )


def sum_col(left_rows, product, out_rows):

    def partial_value(row_start, row_count):
        return product(left_rows)

    return lax.psum_scatter(
        partial_value(jnp.int32(0), out_rows * lax.axis_size("col")),
        "col",
        scatter_dimension=0,
        tiled=True,
    )


def contract_last(row_block, weight_block):
    return lax.dot_general(
        row_block, weight_block, (((1,), (1,)), ((), ())), preferred_element_type=jnp.float32
    )


def token_product(left_rows, right_rows):
    return lax.dot_general(
        left_rows, right_rows, (((0,), (0,)), ((), ())), preferred_element_type=jnp.float32
    )


def weight_grad(left_rows, right_rows):
    return token_product(left_rows, right_rows)


def scale_of(values):
    return lax.rsqrt(feature_sum(jnp.sum(values * values, axis=1)) / MODEL_WIDTH + EPS_NORM)


def norm_back(values, scaled, gain_row, gradient):
    weighted = gain_row * gradient
    inner_sum = feature_sum(jnp.sum(weighted * values, axis=1))
    through = scaled[:, None] * weighted - values * (scaled**3 * inner_sum / MODEL_WIDTH)[:, None]
    gain_part = jnp.sum(gradient * values * scaled[:, None], axis=0)
    return (through, gain_part)


def adamw(current, gradient, first, second, step_rate, decay_rate):
    mean_new = BETA_ONE * first + (1.0 - BETA_ONE) * gradient
    square_new = BETA_TWO * second + (1.0 - BETA_TWO) * gradient * gradient
    mean_hat = mean_new / (1.0 - BETA_ONE**STEP)
    square_hat = square_new / (1.0 - BETA_TWO**STEP)
    updated = current - step_rate * (
        mean_hat / (jnp.sqrt(square_hat) + EPS_ADAM) + decay_rate * current
    )
    return (updated, mean_new, square_new)


def body(
    block_input,
    cotangent,
    norm_gains,
    gains_first,
    gains_second,
    heads_projection_weight,
    heads_first_moment,
    heads_second_moment,
    merge_weight,
    merge_first,
    merge_second,
    gating_weight,
    gating_first,
    gating_second,
    down_weight,
    down_first,
    down_second,
):
    column_count = lax.axis_size("col")
    row_count = lax.axis_size("row")
    local_tokens = block_input.shape[0]
    seq_tokens = local_tokens * column_count
    row_tokens = seq_tokens // row_count
    head_groups = KEY_VALUE_HEADS // column_count
    head_scale = HEAD_SIZE ** (-0.5)
    w_heads, w_merge, w_gating, w_down = (
        lax.all_gather(heads_projection_weight.astype(jnp.bfloat16), "dp", axis=0, tiled=True),
        lax.all_gather(merge_weight.astype(jnp.bfloat16), "dp", axis=0, tiled=True),
        lax.all_gather(gating_weight.astype(jnp.bfloat16), "dp", axis=0, tiled=True),
        lax.all_gather(down_weight.astype(jnp.bfloat16), "dp", axis=0, tiled=True),
    )
    inputs = block_input.astype(jnp.float32)
    gain_one = norm_gains[0]
    gain_two = norm_gains[1]
    scale_one = scale_of(inputs)
    normed_one = (inputs * scale_one[:, None] * gain_one).astype(jnp.bfloat16)
    normed_all = gather_col(normed_one)

    def heads_product(row_block):
        return jnp.dot(row_block, w_heads, preferred_element_type=jnp.float32)

    mixed_token_rows = sum_row(normed_all, heads_product, row_tokens).reshape(
        row_tokens, head_groups, QUERY_PER_GROUP + 2, HEAD_SIZE
    )
    positions = lax.axis_index("row") * row_tokens + jnp.arange(row_tokens, dtype=jnp.int32)
    cosine_rows, sine_rows = rope_tables(positions)
    query_rows = rotate(
        mixed_token_rows[:, :, :QUERY_PER_GROUP],
        cosine_rows[:, None, None],
        sine_rows[:, None, None],
    ).astype(jnp.bfloat16)
    key_rows = rotate(
        mixed_token_rows[:, :, QUERY_PER_GROUP], cosine_rows[:, None], sine_rows[:, None]
    ).astype(jnp.bfloat16)
    value_rows = mixed_token_rows[:, :, QUERY_PER_GROUP + 1].astype(jnp.bfloat16)
    keys_all, values_all = (
        lax.all_gather(
            key_rows.reshape(row_tokens, head_groups * HEAD_SIZE), "row", axis=0, tiled=True
        ),
        lax.all_gather(
            value_rows.reshape(row_tokens, head_groups * HEAD_SIZE), "row", axis=0, tiled=True
        ),
    )
    keys_all = keys_all.reshape(seq_tokens, head_groups, HEAD_SIZE)
    values_all = values_all.reshape(seq_tokens, head_groups, HEAD_SIZE)
    causal = positions[:, None] >= jnp.arange(seq_tokens, dtype=jnp.int32)[None, :]

    def scores_of(queries):
        raw_scores = (
            jnp.einsum("tgqd,sgd->gqts", queries, keys_all, preferred_element_type=jnp.float32)
            * head_scale
        )
        return jnp.where(causal, raw_scores, MASK_FILL)

    scores = scores_of(query_rows)
    row_max = jnp.max(scores, axis=-1, keepdims=True)
    exponent = jnp.exp(scores - row_max)
    exp_total = jnp.sum(exponent, axis=-1, keepdims=True)
    probs_low = (exponent / exp_total).astype(jnp.bfloat16)
    log_total = row_max + jnp.log(exp_total)
    attended = jnp.einsum(
        "gqts,sgd->tgqd", probs_low, values_all, preferred_element_type=jnp.float32
    )
    attended = attended.reshape(row_tokens, head_groups * QUERY_PER_GROUP * HEAD_SIZE).astype(
        jnp.bfloat16
    )
    attended_all = gather_row(attended)

    def merge_product(row_block):
        return jnp.dot(row_block, w_merge, preferred_element_type=jnp.float32)

    middle = inputs + sum_col(attended_all, merge_product, local_tokens)
    scale_two = scale_of(middle)
    normed_two = (middle * scale_two[:, None] * gain_two).astype(jnp.bfloat16)
    normed_two_all = gather_col(normed_two)

    def gating_product(row_block):
        return jnp.einsum("td,dkf->tkf", row_block, w_gating, preferred_element_type=jnp.float32)

    gated = sum_row(normed_two_all, gating_product, row_tokens)
    gate_value = gated[:, 0]
    up_value = gated[:, 1]
    gate_sigmoid = jax.nn.sigmoid(gate_value)
    silu_gate = gate_value * gate_sigmoid
    hidden = (silu_gate * up_value).astype(jnp.bfloat16)
    hidden_all = gather_row(hidden)

    def down_product(row_block):
        return jnp.dot(row_block, w_down, preferred_element_type=jnp.float32)

    block_output = (middle + sum_col(hidden_all, down_product, local_tokens)).astype(jnp.bfloat16)
    grad_output = cotangent.astype(jnp.float32)
    grad_output_all = gather_col(cotangent)
    down_grad = weight_grad(hidden_all, grad_output_all)

    def down_back(row_block):
        return contract_last(row_block, w_down)

    grad_hidden = sum_row(grad_output_all, down_back, row_tokens)
    grad_gate = grad_hidden * up_value * gate_sigmoid * (1.0 + gate_value * (1.0 - gate_sigmoid))
    grad_up = grad_hidden * silu_gate
    grad_gated = jnp.stack([grad_gate, grad_up], axis=1).astype(jnp.bfloat16)
    grad_gated_all = gather_row(grad_gated)
    gating_grad = weight_grad(normed_two_all, grad_gated_all)

    def gating_back(row_block):
        return jnp.einsum("tkf,dkf->td", row_block, w_gating, preferred_element_type=jnp.float32)

    grad_normed_two = sum_col(grad_gated_all, gating_back, local_tokens)
    middle_part, gain_two_grad = norm_back(middle, scale_two, gain_two, grad_normed_two)
    grad_middle = grad_output + middle_part
    grad_branch = grad_middle.astype(jnp.bfloat16)
    grad_branch_all = gather_col(grad_branch)
    merge_grad = weight_grad(attended_all, grad_branch_all)

    def merge_back(row_block):
        return contract_last(row_block, w_merge)

    grad_attended = sum_row(grad_branch_all, merge_back, row_tokens).astype(jnp.bfloat16)
    grad_attended = grad_attended.reshape(row_tokens, head_groups, QUERY_PER_GROUP, HEAD_SIZE)
    soft_again = jnp.exp(scores_of(query_rows) - log_total)
    grad_probs = jnp.einsum(
        "tgqd,sgd->gqts", grad_attended, values_all, preferred_element_type=jnp.float32
    )
    inner_sum = jnp.sum(soft_again * grad_probs, axis=-1, keepdims=True)
    grad_scores = (soft_again * (grad_probs - inner_sum)).astype(jnp.bfloat16)
    grad_query = (
        jnp.einsum("gqts,sgd->tgqd", grad_scores, keys_all, preferred_element_type=jnp.float32)
        * head_scale
    )
    key_part = (
        jnp.einsum("gqts,tgqd->sgd", grad_scores, query_rows, preferred_element_type=jnp.float32)
        * head_scale
    )
    value_part = jnp.einsum(
        "gqts,tgqd->sgd",
        soft_again.astype(jnp.bfloat16),
        grad_attended,
        preferred_element_type=jnp.float32,
    )
    key_summed, value_summed = (
        lax.psum_scatter(
            key_part.reshape(seq_tokens, head_groups * HEAD_SIZE).astype(jnp.bfloat16),
            "row",
            scatter_dimension=0,
            tiled=True,
        ).astype(jnp.float32),
        lax.psum_scatter(
            value_part.reshape(seq_tokens, head_groups * HEAD_SIZE).astype(jnp.bfloat16),
            "row",
            scatter_dimension=0,
            tiled=True,
        ).astype(jnp.float32),
    )
    grad_query = rotate(grad_query, cosine_rows[:, None, None], -sine_rows[:, None, None])
    grad_keys = rotate(
        key_summed.reshape(row_tokens, head_groups, HEAD_SIZE),
        cosine_rows[:, None],
        -sine_rows[:, None],
    )
    grad_mixed = jnp.concatenate(
        [
            grad_query,
            grad_keys[:, :, None],
            value_summed.reshape(row_tokens, head_groups, 1, HEAD_SIZE),
        ],
        axis=2,
    )
    grad_mixed = grad_mixed.reshape(
        row_tokens, head_groups * (QUERY_PER_GROUP + 2) * HEAD_SIZE
    ).astype(jnp.bfloat16)
    grad_mixed_all = gather_row(grad_mixed)
    heads_grad = weight_grad(normed_all, grad_mixed_all)

    def heads_back(row_block):
        return contract_last(row_block, w_heads)

    grad_normed_one = sum_col(grad_mixed_all, heads_back, local_tokens)
    input_part, gain_one_grad = norm_back(inputs, scale_one, gain_one, grad_normed_one)
    input_grad = grad_middle + input_part
    gains_grad = lax.psum(jnp.stack([gain_one_grad, gain_two_grad]), ("dp", "col"))
    heads_grad, merge_grad, gating_grad, down_grad = (
        lax.psum_scatter(
            heads_grad.astype(jnp.bfloat16), "dp", scatter_dimension=0, tiled=True
        ).astype(jnp.float32),
        lax.psum_scatter(
            merge_grad.astype(jnp.bfloat16), "dp", scatter_dimension=0, tiled=True
        ).astype(jnp.float32),
        lax.psum_scatter(
            gating_grad.astype(jnp.bfloat16), "dp", scatter_dimension=0, tiled=True
        ).astype(jnp.float32),
        lax.psum_scatter(
            down_grad.astype(jnp.bfloat16), "dp", scatter_dimension=0, tiled=True
        ).astype(jnp.float32),
    )
    gains_next, gains_mean, gains_square = adamw(
        norm_gains, gains_grad, gains_first, gains_second, RATE_GAIN, 0.0
    )
    heads_next, heads_mean, heads_square = adamw(
        heads_projection_weight,
        heads_grad,
        heads_first_moment,
        heads_second_moment,
        RATE_MATRIX,
        WEIGHT_DECAY,
    )
    merge_next, merge_mean, merge_square = adamw(
        merge_weight, merge_grad, merge_first, merge_second, RATE_MERGE, WEIGHT_DECAY
    )
    gating_next, gating_mean, gating_square = adamw(
        gating_weight, gating_grad, gating_first, gating_second, RATE_MATRIX, WEIGHT_DECAY
    )
    down_next, down_mean, down_square = adamw(
        down_weight, down_grad, down_first, down_second, RATE_MATRIX, WEIGHT_DECAY
    )
    return (
        block_output,
        input_grad,
        gains_grad,
        gains_next,
        gains_mean,
        gains_square,
        heads_grad,
        heads_next,
        heads_mean,
        heads_square,
        merge_grad,
        merge_next,
        merge_mean,
        merge_square,
        gating_grad,
        gating_next,
        gating_mean,
        gating_square,
        down_grad,
        down_next,
        down_mean,
        down_square,
    )


def solution(mesh):
    in_specs = (
        P(("dp", "col"), "row"),
        P(("dp", "col"), "row"),
        P(None, "row"),
        P(None, "row"),
        P(None, "row"),
        P(("row", "dp"), "col"),
        P(("row", "dp"), "col"),
        P(("row", "dp"), "col"),
        P(("col", "dp"), "row"),
        P(("col", "dp"), "row"),
        P(("col", "dp"), "row"),
        P(("row", "dp"), None, "col"),
        P(("row", "dp"), None, "col"),
        P(("row", "dp"), None, "col"),
        P(("col", "dp"), "row"),
        P(("col", "dp"), "row"),
        P(("col", "dp"), "row"),
    )
    out_specs = (
        P(("dp", "col"), "row"),
        P(("dp", "col"), "row"),
        P(None, "row"),
        P(None, "row"),
        P(None, "row"),
        P(None, "row"),
        P(("row", "dp"), "col"),
        P(("row", "dp"), "col"),
        P(("row", "dp"), "col"),
        P(("row", "dp"), "col"),
        P(("col", "dp"), "row"),
        P(("col", "dp"), "row"),
        P(("col", "dp"), "row"),
        P(("col", "dp"), "row"),
        P(("row", "dp"), None, "col"),
        P(("row", "dp"), None, "col"),
        P(("row", "dp"), None, "col"),
        P(("row", "dp"), None, "col"),
        P(("col", "dp"), "row"),
        P(("col", "dp"), "row"),
        P(("col", "dp"), "row"),
        P(("col", "dp"), "row"),
    )
    return jax.shard_map(body, mesh=mesh, in_specs=in_specs, out_specs=out_specs, check_vma=False)
```

profile of v0, /device:TPU:0, one launch (start us, length us, event | category | flops | bytes accessed | tf_op | source)
XLA Modules:
  0.0 1633.1 jit_solution(9358004916800754308)
XLA Ops:
  8.5 7.0 psum.35
  20.5 25.9 %all-gather.13.cloned.1.call-done = bf16[1024,512]{1,0:T(8,128)(2,1)} async-done(((bf16[512,512]{1,0:T(8,128)(2,1)}), bf16[1024,512]{1,0:T(8,128)(2,1)}) %all-gather.13.cloned.1.call-update) | async-done | bytes 1048592 | tf_op jit(solution)/shard_map/all_gather | solution.py:48
  46.4 45.8 %all-gather.15.cloned.1.call-done = bf16[512,1280]{1,0:T(8,128)(2,1)} async-done(((bf16[32,1280]{1,0:T(8,128)(2,1)}), bf16[512,1280]{1,0:T(8,128)(2,1)}) %all-gather.15.cloned.1.call-update) | async-done | bytes 1310736 | tf_op jit(solution)/shard_map/all_gather | solution.py:147
  92.2 5.5 fusion.56
  99.7 51.4 %reduce-scatter.15.cloned.1.call-done = f32[256,1280]{1,0:T(8,128)} async-done(((f32[1024,1280]{1,0:T(8,128)}), f32[256,1280]{1,0:T(8,128)}) %reduce-scatter.15.cloned.1.call-update) | async-done | bytes 1310736 | tf_op jit(solution)/shard_map/reduce_scatter | solution.py:60
  153.1 5.8 all_gather.45
  158.9 5.8 all_gather.44
  164.7 7.2 fusion.55
  171.9 8.0 fusion.3
  179.9 8.3 fusion.13
  188.3 9.3 all-gather.19.cloned.1.call-done
  197.6 29.3 %all-gather.17.cloned.1.call-done = bf16[1024,1024]{0,1:T(8,128)(2,1)} async-done(((bf16[256,1024]{0,1:T(8,128)(2,1)}), bf16[1024,1024]{0,1:T(8,128)(2,1)}) %all-gather.17.cloned.1.call-update) | async-done | bytes 2097168 | tf_op jit(solution)/shard_map/all_gather | solution.py:52
  233.9 35.4 %reduce-scatter.17.cloned.1.call-done = f32[512,512]{1,0:T(8,128)} async-done(((f32[1024,512]{1,0:T(8,128)}), f32[512,512]{1,0:T(8,128)}) %reduce-scatter.17.cloned.1.call-update) | async-done | bytes 1048592 | tf_op jit(solution)/shard_map/reduce_scatter | solution.py:73
  270.7 5.9 psum.36
  277.9 18.0 %all-gather.29.cloned.1.call-done = bf16[1024,512]{1,0:T(8,128)(2,1)} async-done(((bf16[512,512]{1,0:T(8,128)(2,1)}), bf16[1024,512]{1,0:T(8,128)(2,1)}) %all-gather.29.cloned.1.call-update) | async-done | bytes 1048592 | tf_op jit(solution)/shard_map/all_gather | solution.py:48
  295.9 49.7 %all-gather.27.cloned.1.call-done = bf16[2816,512]{1,0:T(8,128)(2,1)} async-done(((bf16[176,512]{1,0:T(8,128)(2,1)}), bf16[2816,512]{1,0:T(8,128)(2,1)}) %all-gather.27.cloned.1.call-update) | async-done | bytes 2883600 | tf_op jit(solution)/shard_map/all_gather | solution.py:150
  345.6 9.6 fusion.59
  355.2 51.3 %all-gather.23.cloned.1.call-done = bf16[512,2,2816]{2,0,1:T(8,128)(2,1)} async-done(((bf16[32,2,2816]{2,0,1:T(8,128)(2,1)}), bf16[512,2,2816]{2,0,1:T(8,128)(2,1)}) %all-gather.23.cloned.1.call-update) | async-done | bytes 5767184 | tf_op jit(solution)/shard_map/all_gather | solution.py:149
  406.5 27.1 %all-gather.21.cloned.1.call-done = bf16[1024,512]{1,0:T(8,128)(2,1)} async-done(((bf16[512,512]{1,0:T(8,128)(2,1)}), bf16[1024,512]{1,0:T(8,128)(2,1)}) %all-gather.21.cloned.1.call-update) | async-done | bytes 1048592 | tf_op jit(solution)/shard_map/all_gather | solution.py:48
  433.6 13.6 fusion.31
  447.3 92.9 %reduce-scatter.23.cloned.1.call-done = f32[256,2816]{1,0:T(8,128)} async-done(((f32[1024,2816]{1,0:T(8,128)}), f32[256,2816]{1,0:T(8,128)}) %reduce-scatter.23.cloned.1.call-update) | async-done | bytes 2883600 | tf_op jit(solution)/shard_map/reduce_scatter | solution.py:60
  540.2 200.7 %reduce-scatter.19.cloned.1.call-done = f32[256,2,2816]{2,0,1:T(8,128)} async-done(((f32[1024,2,2816]{2,0,1:T(8,128)}), f32[256,2,2816]{2,0,1:T(8,128)}) %reduce-scatter.19.cloned.1.call-update) | async-done | bytes 5767184 | tf_op jit(solution)/shard_map/reduce_scatter | solution.py:60
  740.9 5.2 fusion.11
  748.1 106.9 %all-gather.31.cloned.1.call-done = bf16[1024,2,2816]{2,0,1:T(8,128)(2,1)} async-done(((bf16[256,2,2816]{2,0,1:T(8,128)(2,1)}), bf16[1024,2,2816]{2,0,1:T(8,128)(2,1)}) %all-gather.31.cloned.1.call-update) | async-done | bytes 11534352 | tf_op jit(solution)/shard_map/all_gather | solution.py:52
  855.0 11.7 convolution_bitcast_fusion
  866.7 38.5 %reduce-scatter.25.cloned.1.call-done = f32[512,512]{1,0:T(8,128)} async-done(((f32[1024,512]{1,0:T(8,128)}), f32[512,512]{1,0:T(8,128)}) %reduce-scatter.25.cloned.1.call-update) | async-done | bytes 1048592 | tf_op jit(solution)/shard_map/reduce_scatter | solution.py:73
  906.8 6.0 psum.37
  915.2 25.7 %all-gather.33.cloned.1.call-done = bf16[1024,512]{1,0:T(8,128)(2,1)} async-done(((bf16[512,512]{1,0:T(8,128)(2,1)}), bf16[1024,512]{1,0:T(8,128)(2,1)}) %all-gather.33.cloned.1.call-update) | async-done | bytes 1048592 | tf_op jit(solution)/shard_map/all_gather | solution.py:48
  946.0 44.7 %reduce-scatter.27.cloned.1.call-done = f32[256,1024]{1,0:T(8,128)} async-done(((f32[1024,1024]{1,0:T(8,128)}), f32[256,1024]{1,0:T(8,128)}) %reduce-scatter.27.cloned.1.call-update) | async-done | bytes 1048592 | tf_op jit(solution)/shard_map/reduce_scatter | solution.py:60
  994.1 13.5 fusion
  1010.5 10.3 fusion.2
  1020.9 6.7 fusion.21
  1027.7 9.1 fusion.18
  1037.6 5.0 fusion.12
  1046.8 20.3 %reduce-scatter.31.cloned.1.call-done = bf16[256,128]{0,1:T(8,128)(2,1)} async-done(((bf16[1024,128]{0,1:T(8,128)(2,1)}), bf16[256,128]{0,1:T(8,128)(2,1)}) %reduce-scatter.31.cloned.1.call-update) | async-done | bytes 65552 | tf_op jit(solution)/shard_map/reduce_scatter | solution.py:288
  1068.9 59.7 %all-gather.25.cloned.1.call-done = bf16[1024,2816]{1,0:T(8,128)(2,1)} async-done(((bf16[256,2816]{1,0:T(8,128)(2,1)}), bf16[1024,2816]{1,0:T(8,128)(2,1)}) %all-gather.25.cloned.1.call-update) | async-done | bytes 5767184 | tf_op jit(solution)/shard_map/all_gather | solution.py:52
  1128.6 7.7 convolution_convert_fusion.1
  1140.9 12.7 convolution_convert_fusion
  1153.7 11.2 all-gather.35.cloned.1.call-done
  1169.4 5.0 fusion.61
  1174.5 8.0 fusion.58
  1182.5 63.0 %reduce-scatter.41.cloned.1.call-done = bf16[176,512]{1,0:T(8,128)(2,1)} async-done(((bf16[2816,512]{1,0:T(8,128)(2,1)}), bf16[176,512]{1,0:T(8,128)(2,1)}) %reduce-scatter.41.cloned.1.call-update) | async-done | bytes 180240 | tf_op jit(solution)/shard_map/reduce_scatter | solution.py:332
  1247.9 73.7 %reduce-scatter.37.cloned.1.call-done = bf16[64,512]{1,0:T(8,128)(2,1)} async-done(((bf16[1024,512]{1,0:T(8,128)(2,1)}), bf16[64,512]{1,0:T(8,128)(2,1)}) %reduce-scatter.37.cloned.1.call-update) | async-done | bytes 65552 | tf_op jit(solution)/shard_map/reduce_scatter | solution.py:326
  1323.3 81.4 %reduce-scatter.39.cloned.1.call-done = bf16[32,2,2816]{2,0,1:T(8,128)(2,1)} async-done(((bf16[512,2,2816]{2,0,1:T(8,128)(2,1)}), bf16[32,2,2816]{2,0,1:T(8,128)(2,1)}) %reduce-scatter.39.cloned.1.call-update) | async-done | bytes 360464 | tf_op jit(solution)/shard_map/reduce_scatter | solution.py:329
  1412.3 68.5 %reduce-scatter.35.cloned.1.call-done = bf16[32,1280]{1,0:T(8,128)(2,1)} async-done(((bf16[512,1280]{1,0:T(8,128)(2,1)}), bf16[32,1280]{1,0:T(8,128)(2,1)}) %reduce-scatter.35.cloned.1.call-update) | async-done | bytes 81936 | tf_op jit(solution)/shard_map/reduce_scatter | solution.py:323
  1482.6 35.7 %reduce-scatter.33.cloned.1.call-done = f32[512,512]{1,0:T(8,128)} async-done(((f32[1024,512]{1,0:T(8,128)}), f32[512,512]{1,0:T(8,128)}) %reduce-scatter.33.cloned.1.call-update) | async-done | bytes 1048592 | tf_op jit(solution)/shard_map/reduce_scatter | solution.py:73
  1520.0 6.0 psum.38
  1526.0 96.3 %psum.39 = f32[2,512]{1,0:T(2,128)S(1)} all-reduce(f32[2,512]{1,0:T(2,128)S(1)} %pad_maximum_fusion.6), channel_id=1, replica_groups=mesh['dp'=16,'row'=4,'col'=2] {'dp','col'}, use_global_device_ids=true, to_apply=%region_23.24 | all-reduce | flops 1024 | bytes 8192 | tf_op jit(solution)/shard_map/psum | solution.py:321
  (166 shorter events, 72.2 us)
Async XLA Ops:
  7.2 39.2 %all-gather.13.cloned.1.call-start = ((), (), s32[]{:S(2)}) async-start(), calls=%async_computation.14 | async-start | bytes 1572864 | tf_op jit(solution)/shard_map/all_gather | solution.py:48
  16.0 76.2 %copy-start.15 = (f32[512]{0:T(512)}, f32[512]{0:T(512)S(1)}, u32[]{:S(2)}) copy-start(f32[512]{0:T(512)S(1)} %add_rsqrt_fusion.1) | copy-start | bytes 6148
  16.8 75.4 %copy-start.17 = (f32[1,512]{1,0:T(1,128)}, f32[1,512]{1,0:T(1,128)S(1)}, u32[]{:S(2)}) copy-start(f32[1,512]{1,0:T(1,128)S(1)} %get-tuple-element.104) | copy-start | bytes 6148
  18.8 73.3 %all-gather.15.cloned.1.call-start = ((), (), s32[]{:S(2)}) async-start(), calls=%async_computation.15 | async-start | bytes 1392640 | tf_op jit(solution)/shard_map/all_gather | solution.py:147
  20.5 130.6 %reduce-scatter.15.cloned.1.call-start = ((), (), s32[]{:S(2)}) async-start(), calls=%async_computation.16 | async-start | bytes 6553600 | tf_op jit(solution)/shard_map/reduce_scatter | solution.py:60
  97.7 99.9 %all-gather.19.cloned.1.call-start = ((), (), s32[]{:S(2)}) async-start(), calls=%async_computation.18 | async-start | bytes 1114112 | tf_op jit(solution)/shard_map/all_gather | solution.py:148
  99.2 127.7 %all-gather.17.cloned.1.call-start = ((), (), s32[]{:S(2)}) async-start(), calls=%async_computation.17 | async-start | bytes 2621440 | tf_op jit(solution)/shard_map/all_gather | solution.py:52
  164.7 15.2 copy-start.8
  188.2 44.1 %copy-start.5 = (f32[176,512]{1,0:T(8,128)S(1)}, f32[176,512]{1,0:T(8,128)}, u32[]{:S(2)}) copy-start(f32[176,512]{1,0:T(8,128)} %param.31) | copy-start | bytes 1081348
  188.2 44.8 %copy-start.3 = (f32[32,2,2816]{2,1,0:T(2,128)S(1)}, f32[32,2,2816]{2,1,0:T(2,128)}, u32[]{:S(2)}) copy-start(f32[32,2,2816]{2,1,0:T(2,128)} %param.28) | copy-start | bytes 2162692
  188.2 81.1 %copy-start = (bf16[512,512]{1,0:T(8,128)(2,1)S(1)}, bf16[512,512]{1,0:T(8,128)(2,1)}, u32[]{:S(2)}) copy-start(bf16[512,512]{1,0:T(8,128)(2,1)} %param.17) | copy-start | bytes 1572868
  188.2 81.1 %reduce-scatter.17.cloned.1.call-start = ((), (), s32[]{:S(2)}) async-start(), calls=%async_computation.19 | async-start | bytes 3145728 | tf_op jit(solution)/shard_map/reduce_scatter | solution.py:73
  231.4 64.4 %all-gather.29.cloned.1.call-start = ((), (), s32[]{:S(2)}) async-start(), calls=%async_computation.26 | async-start | bytes 1572864 | tf_op jit(solution)/shard_map/all_gather | solution.py:48
  232.2 113.4 %all-gather.27.cloned.1.call-start = ((), (), s32[]{:S(2)}) async-start(), calls=%async_computation.24 | async-start | bytes 3063808 | tf_op jit(solution)/shard_map/all_gather | solution.py:150
  233.0 173.5 %all-gather.23.cloned.1.call-start = ((), (), s32[]{:S(2)}) async-start(), calls=%async_computation.21 | async-start | bytes 6127616 | tf_op jit(solution)/shard_map/all_gather | solution.py:149
  233.8 199.8 %all-gather.21.cloned.1.call-start = ((), (), s32[]{:S(2)}) async-start(), calls=%async_computation.20 | async-start | bytes 1572864 | tf_op jit(solution)/shard_map/all_gather | solution.py:48
  277.7 262.6 %reduce-scatter.23.cloned.1.call-start = ((), (), s32[]{:S(2)}) async-start(), calls=%async_computation.27 | async-start | bytes 14417920 | tf_op jit(solution)/shard_map/reduce_scatter | solution.py:60
  355.2 385.7 %reduce-scatter.19.cloned.1.call-start = ((), (), s32[]{:S(2)}) async-start(), calls=%async_computation.22 | async-start | bytes 28835840 | tf_op jit(solution)/shard_map/reduce_scatter | solution.py:60
  447.3 407.7 %all-gather.31.cloned.1.call-start = ((), (), s32[]{:S(2)}) async-start(), calls=%async_computation.28 | async-start | bytes 14417920 | tf_op jit(solution)/shard_map/all_gather | solution.py:52
  748.0 157.2 %reduce-scatter.25.cloned.1.call-start = ((), (), s32[]{:S(2)}) async-start(), calls=%async_computation.29 | async-start | bytes 3145728 | tf_op jit(solution)/shard_map/reduce_scatter | solution.py:73
  866.7 46.2 %copy-start.2 = (bf16[512,512]{1,0:T(8,128)(2,1)S(1)}, bf16[512,512]{1,0:T(8,128)(2,1)}, u32[]{:S(2)}) copy-start(bf16[512,512]{1,0:T(8,128)(2,1)} %param.18) | copy-start | bytes 1572868
  866.7 74.3 %all-gather.33.cloned.1.call-start = ((), (), s32[]{:S(2)}) async-start(), calls=%async_computation.30 | async-start | bytes 1572864 | tf_op jit(solution)/shard_map/all_gather | solution.py:48
  915.1 75.5 %reduce-scatter.27.cloned.1.call-start = ((), (), s32[]{:S(2)}) async-start(), calls=%async_computation.31 | async-start | bytes 5242880 | tf_op jit(solution)/shard_map/reduce_scatter | solution.py:60
  945.7 100.2 %reduce-scatter.29.cloned.1.call-start = ((), (), s32[]{:S(2)}) async-start(), calls=%async_computation.32 | async-start | bytes 327680 | tf_op jit(solution)/shard_map/reduce_scatter | solution.py:282
  994.0 15.3 slice-start.2
  994.0 16.5 %slice-start.3 = ((s8[16777216]{0:T(1024)(128)(4,1)}), s8[4194304]{0:T(1024)(128)(4,1)S(1)}, s32[]{:S(2)}) async-start(s8[16777216]{0:T(1024)(128)(4,1)} %bitcast.124), calls=%async_computation.43 | async-start | bytes 8388608
  1027.6 39.5 %reduce-scatter.31.cloned.1.call-start = ((), (), s32[]{:S(2)}) async-start(), calls=%async_computation.33 | async-start | bytes 327680 | tf_op jit(solution)/shard_map/reduce_scatter | solution.py:288
  1036.9 91.8 %all-gather.25.cloned.1.call-start = ((), (), s32[]{:S(2)}) async-start(), calls=%async_computation.23 | async-start | bytes 7208960 | tf_op jit(solution)/shard_map/all_gather | solution.py:52
  1037.6 127.3 %all-gather.35.cloned.1.call-start = ((), (), s32[]{:S(2)}) async-start(), calls=%async_computation.34 | async-start | bytes 3276800 | tf_op jit(solution)/shard_map/all_gather | solution.py:52
  1068.8 176.7 %reduce-scatter.41.cloned.1.call-start = ((), (), s32[]{:S(2)}) async-start(), calls=%async_computation.39 | async-start | bytes 3063808 | tf_op jit(solution)/shard_map/reduce_scatter | solution.py:332
  1136.4 185.2 %reduce-scatter.37.cloned.1.call-start = ((), (), s32[]{:S(2)}) async-start(), calls=%async_computation.37 | async-start | bytes 1114112 | tf_op jit(solution)/shard_map/reduce_scatter | solution.py:326
  1140.6 264.1 %reduce-scatter.39.cloned.1.call-start = ((), (), s32[]{:S(2)}) async-start(), calls=%async_computation.38 | async-start | bytes 6127616 | tf_op jit(solution)/shard_map/reduce_scatter | solution.py:329
  1153.6 327.2 %reduce-scatter.35.cloned.1.call-start = ((), (), s32[]{:S(2)}) async-start(), calls=%async_computation.36 | async-start | bytes 1392640 | tf_op jit(solution)/shard_map/reduce_scatter | solution.py:323
  1169.4 348.9 %reduce-scatter.33.cloned.1.call-start = ((), (), s32[]{:S(2)}) async-start(), calls=%async_computation.35 | async-start | bytes 3145728 | tf_op jit(solution)/shard_map/reduce_scatter | solution.py:73
  1174.5 71.1 %copy-start.6 = (f32[176,512]{1,0:T(8,128)S(1)}, f32[176,512]{1,0:T(8,128)}, u32[]{:S(2)}) copy-start(f32[176,512]{1,0:T(8,128)} %param.31) | copy-start | bytes 1081348
  1174.5 448.5 %reduce-scatter.21.cloned.1.call-start = ((), (), s32[]{:S(2)}) async-start(), calls=%async_computation.25 | async-start | bytes 3145728 | tf_op jit(solution)/shard_map/reduce_scatter | solution.py:73
  1182.5 139.1 %copy-start.12 = (f32[64,512]{1,0:T(8,128)S(1)}, f32[64,512]{1,0:T(8,128)}, u32[]{:S(2)}) copy-start(f32[64,512]{1,0:T(8,128)} %param.25) | copy-start | bytes 393220
  1182.5 139.1 %copy-start.14 = (f32[64,512]{1,0:T(8,128)S(1)}, f32[64,512]{1,0:T(8,128)}, u32[]{:S(2)}) copy-start(f32[64,512]{1,0:T(8,128)} %param.26) | copy-start | bytes 393220
  1182.5 222.2 %copy-start.4 = (f32[32,2,2816]{2,1,0:T(2,128)S(1)}, f32[32,2,2816]{2,1,0:T(2,128)}, u32[]{:S(2)}) copy-start(f32[32,2,2816]{2,1,0:T(2,128)} %param.28) | copy-start | bytes 2162692
  1323.3 157.5 %copy-start.10 = (f32[32,1280]{1,0:T(8,128)S(1)}, f32[32,1280]{1,0:T(8,128)}, u32[]{:S(2)}) copy-start(f32[32,1280]{1,0:T(8,128)} %param.22) | copy-start | bytes 491524
  1323.3 157.5 %copy-start.13 = (f32[32,1280]{1,0:T(8,128)S(1)}, f32[32,1280]{1,0:T(8,128)}, u32[]{:S(2)}) copy-start(f32[32,1280]{1,0:T(8,128)} %param.23) | copy-start | bytes 491524
  1406.8 111.5 %copy-start.16 = (f32[512]{0:T(512)S(1)}, f32[512]{0:T(512)}, u32[]{:S(2)}) copy-start(f32[512]{0:T(512)} %copy-done.15) | copy-start | bytes 6148
  1406.8 111.5 %copy-start.18 = (f32[1,512]{1,0:T(1,128)S(1)}, f32[1,512]{1,0:T(1,128)}, u32[]{:S(2)}) copy-start(f32[1,512]{1,0:T(1,128)} %copy-done.17) | copy-start | bytes 6148
  1406.8 215.5 %copy-start.20 = (f32[512]{0:T(512)S(1)}, f32[512]{0:T(512)}, u32[]{:S(2)}) copy-start(f32[512]{0:T(512)} %copy-done.19) | copy-start | bytes 6148
  1406.8 215.5 %copy-start.21 = (f32[2,512]{1,0:T(2,128)S(1)}, f32[2,512]{1,0:T(2,128)}, u32[]{:S(2)}) copy-start(f32[2,512]{1,0:T(2,128)} %param.19) | copy-start | bytes 12292
  1406.8 215.5 %copy-start.23 = (f32[2,512]{1,0:T(2,128)S(1)}, f32[2,512]{1,0:T(2,128)}, u32[]{:S(2)}) copy-start(f32[2,512]{1,0:T(2,128)} %param.20) | copy-start | bytes 12292
  1406.8 215.5 %copy-start.24 = (f32[2,512]{1,0:T(2,128)S(1)}, f32[2,512]{1,0:T(2,128)}, u32[]{:S(2)}) copy-start(f32[2,512]{1,0:T(2,128)} %param.21) | copy-start | bytes 12292
  1406.8 216.1 %copy-start.1 = (f32[512,512]{1,0:T(8,128)S(1)}, f32[512,512]{1,0:T(8,128)}, u32[]{:S(2)}) copy-start(f32[512,512]{1,0:T(8,128)} %reduce-scatter.25.cloned.1.call-done) | copy-start | bytes 3145732
  (8 other events, 54.6 us)
Sparse Core Ops, SparseCore 0:
  19.0 27.4 all-gather.12
  49.2 42.9 all-gather.14
  97.8 53.2 reduce-scatter.14
  153.7 43.8 all-gather.18
  199.7 27.2 all-gather.16
  231.6 37.6 reduce-scatter.16
  271.1 24.7 all-gather.28
  298.9 46.7 all-gather.26
  348.5 57.9 all-gather.22
  408.7 24.8 all-gather.20
  436.2 103.9 reduce-scatter.22
  542.7 198.1 reduce-scatter.18
  748.1 106.7 all-gather.30
  866.8 38.4 reduce-scatter.24
  915.3 25.6 all-gather.32
  945.9 44.7 reduce-scatter.26
  1027.7 18.1 reduce-scatter.28
  1048.9 18.1 reduce-scatter.30
  1068.8 59.8 all-gather.24
  1130.7 34.1 all-gather.34
  1168.2 77.2 reduce-scatter.40
  1249.3 72.2 reduce-scatter.36
  1325.3 79.3 reduce-scatter.38
  1408.1 72.6 reduce-scatter.34
  1483.3 34.9 reduce-scatter.32
  1520.5 36.1 reduce-scatter.20
where the time goes:
time: 1640 us; the launch traced here: 1630 us
  waiting for transfers between devices  1270 us (77%)
  matrix products  141 us (9%)
  blocking collectives  133 us (8%)
  other arithmetic  56.7 us (3%)
    reduce_scatter x4, waiting for transfers between devices, sum_row(): lax.psum_scatter(partial_value(jnp.int32(0), out_rows * lax.axis_size('ro...  390 us
    all_gather x4, waiting for transfers between devices, gather_row(): return lax.all_gather(values, 'row', axis=0, tiled=True)  207 us
    reduce_scatter x4, waiting for transfers between devices, sum_col(): lax.psum_scatter(partial_value(jnp.int32(0), out_rows * lax.axis_size('co...  110 us
    all_gather x4, waiting for transfers between devices, gather_col(): return lax.all_gather(values, 'col', axis=0, tiled=True)  96.7 us
    psum x1, blocking collectives, body(): lax.psum(jnp.stack([gain_one_grad, gain_two_grad]), ('dp', 'col'))  96.3 us
    reduce_scatter x1, waiting for transfers between devices, body(): lax.psum_scatter(gating_grad.astype(jnp.bfloat16), 'dp', scatter_dimensio...  81.4 us
    reduce_scatter x1, waiting for transfers between devices, body(): lax.psum_scatter(merge_grad.astype(jnp.bfloat16), 'dp', scatter_dimension...  73.7 us
    reduce_scatter x1, waiting for transfers between devices, body(): lax.psum_scatter(heads_grad.astype(jnp.bfloat16), 'dp', scatter_dimension...  68.5 us
  transfers between devices with their start and end apart: 26, of which 25 were waited for; matrix products, arithmetic and copies ran while one was open for 8% of the time, Pallas kernels for 0%

commit v1 on v0

v1 whole, which is shorter than its diff:
```python
import functools

import jax
import jax.numpy as jnp
from jax import lax
from jax.experimental import pallas as pl
from jax.experimental.pallas import tpu as pltpu
from jax.sharding import PartitionSpec as P

MODEL_WIDTH = 2048
KEY_VALUE_HEADS = 4
HEAD_SIZE = 64
QUERY_PER_GROUP = 8
STEP = 10


EPS_NORM = 1e-05
BETA_ONE = 0.9
BETA_TWO = 0.95
EPS_ADAM = 1e-08
RATE_MATRIX = 0.05
RATE_MERGE = 0.5
RATE_GAIN = 1.0
WEIGHT_DECAY = 0.1
ROPE_BASE = 10000.0
MASK_FILL = -1e30

MESH = pl.DeviceIdType.MESH
VMEM_BYTES = 60 * 2**20
BF16 = jnp.bfloat16
F32 = jnp.float32

SEQ = 1024
OWN = 128
HEADS_COLS = 384
HIDDEN = 768
PIECE = 48
PIECE_USED = 44


class Place:
    def __init__(self):
        self.dp = lax.axis_index("dp")
        self.row = lax.axis_index("row")
        self.col = lax.axis_index("col")
        self.y = lax.div(self.dp, 4)
        self.z = lax.rem(self.dp, 4)
        self.core = lax.rem(self.row, 2)
        self.x = self.col * 2 + lax.div(self.row, 2)

    def near(self, x=0, core=0, y=0, z=0):
        new_x = lax.rem(self.x + x + 4, 4)
        new_core = lax.rem(self.core + core, 2)
        new_y = lax.rem(self.y + y + 4, 4)
        new_z = lax.rem(self.z + z + 4, 4)
        return {
            "dp": new_y * 4 + new_z,
            "row": lax.rem(new_x, 2) * 2 + new_core,
            "col": lax.div(new_x, 2),
        }

    def slot(self, first_axis, first, second):
        y, z = (first, second) if first_axis == "y" else (second, first)
        return lax.rem(self.y + y + 4, 4) * 4 + lax.rem(self.z + z + 4, 4)

    def line(self, x, core):
        return lax.rem(self.x + x + 4, 4) * 2 + lax.rem(self.core + core, 2)

    def peer(self, step):
        other = lax.rem(self.row + step, 4)
        return other, {"dp": self.dp, "row": other, "col": self.col}


class Wires:
    def __init__(self, send, recv, local):
        self.send, self.recv, self.local = send, recv, local
        self.count = 0
        self.local_count = 0
        self.sent = []
        self.kept = []

    def push(self, source, target, device):
        index = self.count
        self.count += 1
        copy = pltpu.make_async_remote_copy(
            src_ref=source,
            dst_ref=target,
            send_sem=self.send.at[index],
            recv_sem=self.recv.at[index],
            device_id=device,
            device_id_type=MESH,
        )
        copy.start()
        self.sent.append(copy)
        return copy

    def keep(self, source, target):
        copy = pltpu.make_async_copy(source, target, self.local.at[self.local_count])
        self.local_count += 1
        copy.start()
        return copy

    def drain(self):
        for copy in self.sent:
            copy.wait_send()


def meet(devices, more=0):
    barrier = pltpu.get_barrier_semaphore()
    for device in devices:
        pl.semaphore_signal(barrier, inc=1, device_id=device, device_id_type=MESH)
    pl.semaphore_wait(barrier, len(devices))


def interleave(*plans):
    waiting = [[next(plan), order, plan] for order, plan in enumerate(plans)]
    while waiting:
        waiting.sort(key=lambda entry: (entry[0], entry[1]))
        entry = waiting[0]
        try:
            entry[0] = max(entry[0], next(entry[2]))
        except StopIteration:
            waiting.pop(0)


def ring_neighbours(place):
    return [place.near(y=1), place.near(y=-1), place.near(z=1), place.near(z=-1)]


def line_neighbours(place):
    return [place.near(x=1), place.near(x=-1), place.near(core=1)]


def line_gather(place, wires, own, out, block, half, start, cost):
    me = place.line(0, 0)
    yield start
    kept = wires.keep(own, block(out, me))
    right = wires.push(own, block(out, me), place.near(x=1))
    left = wires.push(own, block(out, me), place.near(x=-1))
    beside = [wires.push(own, block(out, me), place.near(core=1))]
    yield start + cost + 2
    right.wait_recv()
    came = place.line(-1, 0)
    far_right = wires.push(half(out, came, 0), half(out, came, 0), place.near(x=1))
    beside.append(wires.push(block(out, came), block(out, came), place.near(core=1)))
    left.wait_recv()
    came = place.line(1, 0)
    far_left = wires.push(half(out, came, 1), half(out, came, 1), place.near(x=-1))
    beside.append(wires.push(block(out, came), block(out, came), place.near(core=1)))
    yield start + 1.5 * cost + 4
    far_right.wait_recv()
    far_left.wait_recv()
    came = place.line(2, 0)
    beside.append(wires.push(block(out, came), block(out, came), place.near(core=1)))
    yield start + 1.5 * cost + 6
    kept.wait()
    for copy in beside:
        copy.wait_recv()


def token_block(ref, index):
    return ref.at[pl.ds(pl.multiple_of(index * OWN, OWN), OWN)]


def token_half(ref, index, side):
    return ref.at[pl.ds(pl.multiple_of(index * OWN + side * (OWN // 2), OWN // 2), OWN // 2)]


def tile_block(ref, index):
    x, core = lax.div(index, 2), lax.rem(index, 2)
    rows = pl.ds(pl.multiple_of(lax.div(x, 2) * 512, 512), 512)
    columns = pl.ds(pl.multiple_of((lax.rem(x, 2) * 2 + core) * 512, 512), 512)
    return ref.at[rows, columns]


def tile_half(ref, index, side):
    x, core = lax.div(index, 2), lax.rem(index, 2)
    rows = pl.ds(pl.multiple_of(lax.div(x, 2) * 512 + side * 256, 256), 256)
    columns = pl.ds(pl.multiple_of((lax.rem(x, 2) * 2 + core) * 512, 512), 512)
    return ref.at[rows, columns]


def add_rows(out, terms, rows, step=16):
    def chunk(index, carry):
        at = pl.ds(pl.multiple_of(index * step, step), step)
        out[at, :] = functools.reduce(
            lambda a, b: a + b, [term[at, :].astype(F32) for term in terms]
        ).astype(out.dtype)
        return carry

    lax.fori_loop(0, rows // step, chunk, 0)


LINE_SCATTER_SCRATCH = [
    pltpu.VMEM((4, OWN, MODEL_WIDTH), BF16),
    pltpu.VMEM((2, OWN // 2, MODEL_WIDTH), BF16),
    pltpu.VMEM((2, OWN, MODEL_WIDTH), BF16),
    pltpu.VMEM((3, OWN, MODEL_WIDTH), BF16),
]


def line_scatter(place, wires, part, scratch, start, cost):
    beside, halves, full, total = scratch
    yield start
    pairs = {}
    for offset in (2, 1, 3, 0):
        pairs[offset] = wires.push(
            token_block(part, place.line(offset, 1)), beside.at[offset], place.near(core=1)
        )
    yield start + 2
    pairs[2].wait_recv()
    add_rows(total.at[2], [token_block(part, place.line(2, 0)), beside.at[2]], OWN)
    far_right = wires.push(
        total.at[2, pl.ds(0, OWN // 2)], halves.at[0], place.near(x=1)
    )
    far_left = wires.push(
        total.at[2, pl.ds(OWN // 2, OWN // 2)], halves.at[1], place.near(x=-1)
    )
    yield start + 3
    pairs[1].wait_recv()
    add_rows(total.at[0], [token_block(part, place.line(1, 0)), beside.at[1]], OWN)
    right_late = wires.push(
        total.at[0, pl.ds(OWN // 2, OWN // 2)],
        full.at[0, pl.ds(OWN // 2, OWN // 2)],
        place.near(x=1),
    )
    pairs[3].wait_recv()
    add_rows(total.at[1], [token_block(part, place.line(3, 0)), beside.at[3]], OWN)
    left_late = wires.push(
        total.at[1, pl.ds(0, OWN // 2)], full.at[1, pl.ds(0, OWN // 2)], place.near(x=-1)
    )
    yield start + 5 + 0.5 * cost
    far_right.wait_recv()
    first = total.at[0, pl.ds(0, OWN // 2)]
    add_rows(first, [first, halves.at[0]], OWN // 2)
    right = wires.push(first, full.at[0, pl.ds(0, OWN // 2)], place.near(x=1))
    far_left.wait_recv()
    second = total.at[1, pl.ds(OWN // 2, OWN // 2)]
    add_rows(second, [second, halves.at[1]], OWN // 2)
    left = wires.push(second, full.at[1, pl.ds(OWN // 2, OWN // 2)], place.near(x=-1))
    yield start + 6 + 1.5 * cost
    pairs[0].wait_recv()
    right_late.wait_recv()
    left_late.wait_recv()
    right.wait_recv()
    left.wait_recv()


def scatter_terms(place, part, scratch):
    beside, halves, full, total = scratch
    return [token_block(part, place.line(0, 0)), beside.at[0], full.at[0], full.at[1]]


class Rows:
    def __init__(self, columns):
        self.item_shape = (2, 32, columns)
        self.half_shape = (1, 32, columns)

    def item(self, ref, side, slot):
        return ref.at[pl.ds(2 * side, 2), slot]

    def half(self, ref, side, part, slot):
        return ref.at[pl.ds(2 * side + part, 1), slot]

    def cut(self, item, part):
        return item.at[pl.ds(part, 1)]


class Flat:
    def __init__(self):
        self.item_shape = (PIECE, MODEL_WIDTH // 2)
        self.half_shape = (PIECE, MODEL_WIDTH // 4)

    def item(self, ref, side, slot):
        rows = pl.ds(pl.multiple_of(slot * PIECE, PIECE), PIECE)
        return ref.at[rows, pl.ds(side * (MODEL_WIDTH // 2), MODEL_WIDTH // 2)]

    def half(self, ref, side, part, slot):
        rows = pl.ds(pl.multiple_of(slot * PIECE, PIECE), PIECE)
        return ref.at[rows, pl.ds((2 * side + part) * (MODEL_WIDTH // 4), MODEL_WIDTH // 4)]

    def cut(self, item, part):
        return item.at[:, pl.ds(part * (MODEL_WIDTH // 4), MODEL_WIDTH // 4)]


def ring_move(place, axis, step):
    return place.near(y=step) if axis == "y" else place.near(z=step)


def ring_gather(place, wires, kind, out, side, start, cost):
    first, second = ("z", "y") if side == 0 else ("y", "z")
    slot = functools.partial(place.slot, first)
    spread = {}

    def send_on(offset):
        item = kind.item(out, side, slot(offset, 0))
        spread[offset] = [
            wires.push(item, item, ring_move(place, second, step)) for step in (1, -1)
        ]

    def pass_on(offset):
        right, left = spread[offset]
        right.wait_recv()
        piece = kind.half(out, side, 0, slot(offset, -1))
        one = wires.push(piece, piece, ring_move(place, second, 1))
        left.wait_recv()
        piece = kind.half(out, side, 1, slot(offset, 1))
        return [one, wires.push(piece, piece, ring_move(place, second, -1))]

    yield start
    own = kind.item(out, side, slot(0, 0))
    right = wires.push(own, own, ring_move(place, first, 1))
    left = wires.push(own, own, ring_move(place, first, -1))
    send_on(0)
    yield start + cost + 2
    right.wait_recv()
    piece = kind.half(out, side, 0, slot(-1, 0))
    far_right = wires.push(piece, piece, ring_move(place, first, 1))
    send_on(-1)
    left.wait_recv()
    piece = kind.half(out, side, 1, slot(1, 0))
    far_left = wires.push(piece, piece, ring_move(place, first, -1))
    send_on(1)
    last = []
    yield start + 2 * cost + 4
    last += pass_on(0)
    yield start + 2.5 * cost + 4
    far_right.wait_recv()
    far_left.wait_recv()
    send_on(2)
    yield start + 4 * cost + 4
    last += pass_on(-1)
    yield start + 5.5 * cost + 4
    last += pass_on(1)
    yield start + 6.5 * cost + 4
    last += pass_on(2)
    yield start + 7.5 * cost + 6
    for copy in last:
        copy.wait_recv()


def ring_scatter_scratch(kind):
    def stack(count, shape):
        return pltpu.VMEM((count, *shape), BF16)

    one_side = [
        stack(8, kind.half_shape),
        stack(8, kind.item_shape),
        stack(8, kind.item_shape),
        stack(4, kind.item_shape),
        stack(2, kind.half_shape),
        stack(2, kind.item_shape),
        stack(2, kind.item_shape),
    ]
    return one_side + one_side


def add_item(out, terms):
    out[...] = functools.reduce(lambda a, b: a + b, [t[...].astype(F32) for t in terms]).astype(
        out.dtype
    )


def ring_scatter(place, wires, kind, part, side, scratch, result, start, cost):
    far, sums, came, column, far_last, sums_last, came_last = scratch[7 * side : 7 * side + 7]
    first, second = ("z", "y") if side == 0 else ("y", "z")
    slot = functools.partial(place.slot, first)
    order = (2, 1, -1, 0)
    yield start
    right, left = {}, {}
    for n, offset in enumerate(order):
        target = slot(offset, 2)
        right[offset] = wires.push(
            kind.half(part, side, 0, target), far.at[2 * n], ring_move(place, second, 1)
        )
        left[offset] = wires.push(
            kind.half(part, side, 1, target), far.at[2 * n + 1], ring_move(place, second, -1)
        )

    def add_far(source, halves, out, way):
        keep = 1 - way
        add_item(kind.cut(out, way), [kind.cut(source, way), halves])
        held = kind.cut(out, keep)
        held[...] = kind.cut(source, keep)[...]

    moved = {}
    for n, offset in enumerate(order):
        yield start + 2.5 + (0.5 + n) * cost
        right[offset].wait_recv()
        add_far(kind.item(part, side, slot(offset, 1)), far.at[2 * n], sums.at[2 * n], 0)
        one = wires.push(sums.at[2 * n], came.at[2 * n], ring_move(place, second, 1))
        left[offset].wait_recv()
        add_far(kind.item(part, side, slot(offset, -1)), far.at[2 * n + 1], sums.at[2 * n + 1], 1)
        two = wires.push(sums.at[2 * n + 1], came.at[2 * n + 1], ring_move(place, second, -1))
        moved[offset] = (one, two)

    def finish(n, offset):
        for copy in moved[offset]:
            copy.wait_recv()
        add_item(
            column.at[n],
            [kind.item(part, side, slot(offset, 0)), came.at[2 * n], came.at[2 * n + 1]],
        )

    yield start + 4 + 3 * cost
    finish(0, 2)
    far_right = wires.push(kind.cut(column.at[0], 0), far_last.at[0], ring_move(place, first, 1))
    far_left = wires.push(kind.cut(column.at[0], 1), far_last.at[1], ring_move(place, first, -1))
    yield start + 4 + 4 * cost
    finish(1, 1)
    yield start + 4 + 5 * cost
    finish(2, -1)
    far_right.wait_recv()
    add_far(column.at[1], far_last.at[0], sums_last.at[0], 0)
    one = wires.push(sums_last.at[0], came_last.at[0], ring_move(place, first, 1))
    far_left.wait_recv()
    add_far(column.at[2], far_last.at[1], sums_last.at[1], 1)
    two = wires.push(sums_last.at[1], came_last.at[1], ring_move(place, first, -1))
    yield start + 5 + 6 * cost
    finish(3, 0)
    yield start + 8 + 7.5 * cost
    one.wait_recv()
    two.wait_recv()
    add_item(result, [column.at[3], came_last.at[0], came_last.at[1]])


def call(kernel, outs, ins, scratch, wires, name, cost):
    return pl.pallas_call(
        kernel,
        out_shape=[shape for shape, _ in outs],
        in_specs=[pl.BlockSpec(memory_space=space) for _, space in ins],
        out_specs=[pl.BlockSpec(memory_space=space) for _, space in outs],
        scratch_shapes=list(scratch)
        + [
            pltpu.SemaphoreType.DMA((wires,)),
            pltpu.SemaphoreType.DMA((wires,)),
            pltpu.SemaphoreType.DMA((16,)),
        ],
        compiler_params=pltpu.CompilerParams(
            collective_id=name, has_side_effects=True, vmem_limit_bytes=VMEM_BYTES
        ),
        cost_estimate=pl.CostEstimate(flops=0, bytes_accessed=cost, transcendentals=0),
    )(*[array for array, _ in ins])


def shape(*extent, dtype=BF16):
    return jax.ShapeDtypeStruct(extent, dtype)


def merge_devices(place):
    homes = [
        {"dp": place.row * 4 + z, "row": jnp.int32(row), "col": place.col}
        for z in range(4)
        for row in range(4)
    ]
    users = [{"dp": jnp.int32(dp), "row": place.y, "col": place.col} for dp in range(16)]
    return homes, users


def start_kernel(
    heads_own, gating_own, down_own, merge_own, input_own, gains_own,
    heads, gating, down, merge, inputs, gains,
    send, recv, local,
):
    place = Place()
    wires = Wires(send, recv, local)
    homes, users = merge_devices(place)
    peers = [place.peer(step) for step in (1, 2, 3)]
    same = place.row == place.y
    barrier = pltpu.get_barrier_semaphore()
    devices = ring_neighbours(place) + line_neighbours(place) + [p for _, p in peers]
    for device in devices:
        pl.semaphore_signal(barrier, inc=1, device_id=device, device_id_type=MESH)
    for index, device in enumerate(homes):
        alone = (device["dp"] == place.dp) & (device["row"] == place.row)

        @pl.when(jnp.logical_not(alone))
        def _():
            pl.semaphore_signal(barrier, inc=1, device_id=device, device_id_type=MESH)

    pl.semaphore_wait(barrier, len(devices) + 16 - same.astype(jnp.int32))

    def down_columns(ref, row):
        return ref.at[:, pl.ds(pl.multiple_of(row * 512, 512), 512)]

    def exchange():
        yield 0.0
        moved = []
        kept = wires.keep(heads_own.at[place.row], heads.at[place.row, place.dp])
        for other, device in peers:
            moved.append(
                wires.push(heads_own.at[other], heads.at[place.row, place.dp], device)
            )
        for other, device in peers:
            moved.append(wires.push(gains_own, gains.at[place.row], device))
        kept_gains = wires.keep(gains_own, gains.at[place.row])
        yield 0.2
        rest = [
            wires.keep(gating_own.at[place.row], gating.at[place.row]),
            wires.keep(down_own.at[place.row], down_columns(down, place.row)),
        ]
        later = []
        for other, device in peers:
            later.append(wires.push(gating_own.at[other], gating.at[place.row], device))
            later.append(
                wires.push(down_own.at[other], down_columns(down, place.row), device)
            )
        yield 4.0
        kept.wait()
        kept_gains.wait()
        for copy in moved:
            copy.wait_recv()
        sides = [
            ring_gather(place, wires, Rows(HEADS_COLS), heads, side, 4.1, 1.1) for side in (0, 1)
        ]
        pending = [(next(plan), plan) for plan in sides]
        while pending:
            pending.sort(key=lambda entry: entry[0])
            when, plan = pending[0]
            yield when
            try:
                pending[0] = (next(plan), plan)
            except StopIteration:
                pending.pop(0)
        yield 30.0
        for copy in rest:
            copy.wait()
        for copy in later:
            copy.wait_recv()

    def merge_rows():
        yield 0.15
        target = merge.at[
            pl.ds(pl.multiple_of(place.z * 64, 64), 64),
            pl.ds(pl.multiple_of(place.row * 512, 512), 512),
        ]
        base = wires.count
        wires.count += 16
        copies = []
        for index, device in enumerate(users):
            copy = pltpu.make_async_remote_copy(
                src_ref=merge_own,
                dst_ref=target,
                send_sem=wires.send.at[base + index],
                recv_sem=wires.recv.at[base + place.row * 4 + place.z],
                device_id=device,
                device_id_type=MESH,
            )
            here = pltpu.make_async_copy(
                merge_own, target, wires.recv.at[base + place.row * 4 + place.z]
            )
            alone = (device["dp"] == place.dp) & same
            copies.append((copy, alone))

            @pl.when(alone)
            def _():
                here.start()

            @pl.when(jnp.logical_not(alone))
            def _():
                copy.start()

        yield 28.0
        for index in range(16):
            pltpu.make_async_copy(merge_own, target, wires.recv.at[base + index]).wait()
        for copy, alone in copies:

            @pl.when(jnp.logical_not(alone))
            def _():
                copy.wait_send()

    interleave(
        exchange(),
        merge_rows(),
        line_gather(place, wires, input_own, inputs, tile_block, tile_half, 0.1, 11.4),
    )
    wires.drain()


def middle_kernel(
    part, input_rows, gains, gating_own, down_own, back_own,
    middle, normed, gating, down, back,
    *scratch,
):
    line_scratch, (normed_own, send, recv, local) = scratch[:4], scratch[4:]
    place = Place()
    wires = Wires(send, recv, local)
    meet(ring_neighbours(place) + line_neighbours(place))

    def main():
        yield from line_scatter(place, wires, part, line_scratch, 0.0, 11.4)
        terms = scatter_terms(place, part, line_scratch)

        def chunk(index, carry):
            at = pl.ds(pl.multiple_of(index * 16, 16), 16)
            total = functools.reduce(lambda a, b: a + b, [t[at, :].astype(F32) for t in terms])
            total = total + input_rows[at, :].astype(F32)
            middle[at, :] = total
            scale = lax.rsqrt(
                jnp.sum(total * total, axis=1, keepdims=True) / MODEL_WIDTH + EPS_NORM
            )
            normed_own[at, :] = (total * scale * gains[1:2, :]).astype(BF16)
            return carry

        lax.fori_loop(0, OWN // 16, chunk, 0)
        yield from line_gather(
            place, wires, normed_own, normed, token_block, token_half, 25.0, 11.4
        )

    def weights():
        yield 0.3
        kept = [
            wires.keep(gating_own.at[r], gating.at[r, place.dp]) for r in range(4)
        ]
        rows = pl.ds(pl.multiple_of(place.dp * PIECE, PIECE), PIECE)
        kept.append(wires.keep(down_own, down.at[rows]))
        for copy in kept:
            copy.wait()
        plans = [
            ring_gather(place, wires, Rows(2 * HIDDEN), gating, side, 0.5, 4.3) for side in (0, 1)
        ] + [ring_gather(place, wires, Flat(), down, side, 0.6, 4.3) for side in (0, 1)]
        pending = [(next(plan), order, plan) for order, plan in enumerate(plans)]
        while pending:
            pending.sort(key=lambda entry: entry[:2])
            when, order, plan = pending[0]
            yield when
            try:
                pending[0] = (max(when, next(plan)), order, plan)
            except StopIteration:
                pending.pop(0)

    interleave(
        main(),
        weights(),
        line_gather(place, wires, back_own, back, tile_block, tile_half, 25.5, 22.0),
    )
    wires.drain()


def branch_kernel(
    part, middle, back_rows, gains, gating_part, down_part,
    grad_middle, branch, gain_part, gating_sum, down_sum,
    *scratch,
):
    line_scratch, scratch = scratch[:4], scratch[4:]
    gating_scratch, scratch = scratch[:14], scratch[14:]
    down_scratch, scratch = scratch[:14], scratch[14:]
    branch_own, send, recv, local = scratch
    place = Place()
    wires = Wires(send, recv, local)
    meet(ring_neighbours(place) + line_neighbours(place))

    def main():
        yield from line_scatter(place, wires, part, line_scratch, 0.0, 11.4)
        terms = scatter_terms(place, part, line_scratch)
        gain_part[...] = jnp.zeros_like(gain_part)

        def chunk(index, carry):
            at = pl.ds(pl.multiple_of(index * 16, 16), 16)
            grad = functools.reduce(lambda a, b: a + b, [t[at, :].astype(F32) for t in terms])
            through, gain = norm_back(middle[at, :], gains[1:2, :], grad)
            total = back_rows[at, :].astype(F32) + through
            grad_middle[at, :] = total
            branch_own[at, :] = total.astype(BF16)
            gain_part[...] += gain.reshape(2, 8, MODEL_WIDTH).sum(axis=0)
            return carry

        lax.fori_loop(0, OWN // 16, chunk, 0)
        yield from line_gather(
            place, wires, branch_own, branch, token_block, token_half, 25.0, 11.4
        )

    rows = Rows(2 * HIDDEN)
    flat = Flat()
    interleave(
        main(),
        *[
            ring_scatter(
                place, wires, rows, gating_part, side, gating_scratch,
                gating_sum.at[pl.ds(2 * side, 2)], 0.5, 4.3,
            )
            for side in (0, 1)
        ],
        *[
            ring_scatter(
                place, wires, flat, down_part, side, down_scratch,
                down_sum.at[:, pl.ds(side * 1024, 1024)], 0.6, 4.3,
            )
            for side in (0, 1)
        ],
    )
    wires.drain()


def norm_back(values, gain_row, gradient):
    scale = lax.rsqrt(jnp.sum(values * values, axis=1, keepdims=True) / MODEL_WIDTH + EPS_NORM)
    weighted = gain_row * gradient
    inner = jnp.sum(weighted * values, axis=1, keepdims=True)
    through = scale * weighted - values * (scale * scale * scale * inner / MODEL_WIDTH)
    return through, gradient * values * scale


def finish_kernel(
    part, down_out, middle, grad_middle, input_rows, gains, gain_part,
    heads_part, merge_part, gating_sum, down_sum,
    output, input_grad, gains_grad, heads_pieces, merge_pieces, gating_pieces, down_pieces,
    *scratch,
):
    line_scratch, scratch = scratch[:4], scratch[4:]
    out_scratch, scratch = scratch[:4], scratch[4:]
    heads_scratch, scratch = scratch[:14], scratch[14:]
    (
        heads_sum, output_own, input_grad_own, gain_rows, gain_came, gain_all, send, recv, local,
    ) = scratch
    place = Place()
    wires = Wires(send, recv, local)
    homes, users = merge_devices(place)
    peers = [place.peer(step) for step in (1, 2, 3)]
    same = place.row == place.y
    barrier = pltpu.get_barrier_semaphore()
    devices = ring_neighbours(place) + line_neighbours(place) + [p for _, p in peers]
    for device in devices:
        pl.semaphore_signal(barrier, inc=1, device_id=device, device_id_type=MESH)
    for device in users:
        alone = (device["dp"] == place.dp) & same

        @pl.when(jnp.logical_not(alone))
        def _():
            pl.semaphore_signal(barrier, inc=1, device_id=device, device_id_type=MESH)

    def far(step):
        index = lax.rem(place.col * 16 + place.dp + step, 32)
        return {"dp": lax.rem(index, 16), "row": place.row, "col": lax.div(index, 16)}

    def greet(step, carry):
        pl.semaphore_signal(barrier, inc=1, device_id=far(step), device_id_type=MESH)
        return carry

    lax.fori_loop(1, 32, greet, 0)
    pl.semaphore_wait(barrier, len(devices) + 31 + 16 - same.astype(jnp.int32))

    def column_block(ref, row):
        return ref.at[:, pl.ds(pl.multiple_of(row * 512, 512), 512)]

    def own_rows(ref, row):
        return ref.at[pl.ds(pl.multiple_of(row * OWN, OWN), OWN)]

    def recut(own, out, when):
        kept = wires.keep(column_block(own, place.row), own_rows(out, place.row))
        moved = [
            wires.push(column_block(own, other), own_rows(out, place.row), device)
            for other, device in peers
        ]
        yield when
        kept.wait()
        for copy in moved:
            copy.wait_recv()

    def gradient():
        yield from line_scatter(place, wires, part, line_scratch, 0.0, 11.4)
        terms = scatter_terms(place, part, line_scratch)
        gain_rows[0] = jnp.zeros((8, MODEL_WIDTH), F32)
        gain_rows[1] = gain_part[...]

        def chunk(index, carry):
            at = pl.ds(pl.multiple_of(index * 16, 16), 16)
            grad = functools.reduce(lambda a, b: a + b, [t[at, :].astype(F32) for t in terms])
            through, gain = norm_back(input_rows[at, :].astype(F32), gains[0:1, :], grad)
            input_grad_own[at, :] = grad_middle[at, :] + through
            gain_rows[0] += gain.reshape(2, 8, MODEL_WIDTH).sum(axis=0)
            return carry

        lax.fori_loop(0, OWN // 16, chunk, 0)
        moved = []
        for other, device in peers:
            piece = gain_rows.at[:, :, pl.ds(pl.multiple_of(other * 512, 512), 512)]
            moved.append(wires.push(piece, gain_came.at[place.row], device))
        piece = gain_rows.at[:, :, pl.ds(pl.multiple_of(place.row * 512, 512), 512)]
        kept = wires.keep(piece, gain_came.at[place.row])
        waits = recut(input_grad_own, input_grad, 38.0)
        next(waits)
        yield 28.0
        kept.wait()
        for copy in moved:
            copy.wait_recv()
        local_sum = gain_came[0] + gain_came[1] + gain_came[2] + gain_came[3]
        me = place.col * 16 + place.dp
        gain_all[me] = jnp.concatenate(
            [jnp.sum(local_sum, axis=1), jnp.zeros((6, 512), F32)], axis=0
        )
        base = wires.count
        wires.count += 32

        def gain_copy(step):
            return pltpu.make_async_remote_copy(
                src_ref=gain_all.at[me],
                dst_ref=gain_all.at[me],
                send_sem=wires.send.at[base + step],
                recv_sem=wires.recv.at[base + step],
                device_id=far(step),
                device_id_type=MESH,
            )

        def start(step, carry):
            gain_copy(step).start()
            return carry

        def finish(step, carry):
            gain_copy(step).wait()
            return carry

        lax.fori_loop(1, 32, start, 0)
        yield 36.0
        lax.fori_loop(1, 32, finish, 0)
        gains_grad[...] = functools.reduce(lambda a, b: a + b, [gain_all[i] for i in range(32)])
        yield 38.0
        for _ in waits:
            pass

    def outputs():
        yield from line_scatter(place, wires, down_out, out_scratch, 0.3, 22.0)
        terms = scatter_terms(place, down_out, out_scratch)

        def chunk(index, carry):
            at = pl.ds(pl.multiple_of(index * 16, 16), 16)
            total = functools.reduce(lambda a, b: a + b, [t[at, :].astype(F32) for t in terms])
            output_own[at, :] = (total + middle[at, :]).astype(BF16)
            return carry

        lax.fori_loop(0, OWN // 16, chunk, 0)
        yield from recut(output_own, output, 45.0)

    def back_pieces(part_of, out, when):
        kept = wires.keep(part_of(place.row), out.at[place.row])
        moved = [
            wires.push(part_of(other), out.at[place.row], device) for other, device in peers
        ]
        yield when
        kept.wait()
        for copy in moved:
            copy.wait_recv()

    def heads():
        plans = [
            ring_scatter(
                place, wires, Rows(HEADS_COLS), heads_part, side, heads_scratch,
                heads_sum.at[pl.ds(2 * side, 2)], 0.2, 1.1,
            )
            for side in (0, 1)
        ]
        pending = [(next(plan), order, plan) for order, plan in enumerate(plans)]
        while pending:
            pending.sort(key=lambda entry: entry[:2])
            when, order, plan = pending[0]
            yield when
            try:
                pending[0] = (max(when, next(plan)), order, plan)
            except StopIteration:
                pending.pop(0)
        yield 18.0
        yield from back_pieces(lambda row: heads_sum.at[row], heads_pieces, 40.0)

    def gating():
        yield 0.4
        yield from back_pieces(lambda row: gating_sum.at[row], gating_pieces, 41.0)

    def down():
        yield 0.5
        yield from back_pieces(lambda row: column_block(down_sum, row), down_pieces, 41.0)

    def merge():
        yield 0.1
        base = wires.count
        wires.count += 32
        copies = []
        for index, device in enumerate(homes):
            z, row = index // 4, index % 4
            source = merge_part.at[pl.ds(z * 64, 64), pl.ds(row * 512, 512)]
            copy = pltpu.make_async_remote_copy(
                src_ref=source,
                dst_ref=merge_pieces.at[place.dp],
                send_sem=wires.send.at[base + index],
                recv_sem=wires.recv.at[base + 16 + place.dp],
                device_id=device,
                device_id_type=MESH,
            )
            here = pltpu.make_async_copy(
                source, merge_pieces.at[place.dp], wires.recv.at[base + 16 + place.dp]
            )
            alone = (device["dp"] == place.dp) & (device["row"] == place.row)
            copies.append((copy, alone))

            @pl.when(alone)
            def _():
                here.start()

            @pl.when(jnp.logical_not(alone))
            def _():
                copy.start()

        yield 42.0
        for index in range(16):
            pltpu.make_async_copy(
                merge_part.at[pl.ds(0, 64), pl.ds(0, 512)],
                merge_pieces.at[index],
                wires.recv.at[base + 16 + index],
            ).wait()
        for copy, alone in copies:

            @pl.when(jnp.logical_not(alone))
            def _():
                copy.wait_send()

    interleave(gradient(), outputs(), heads(), gating(), down(), merge())
    wires.drain()


def rope_tables(positions):
    half_width = HEAD_SIZE // 2
    frequency = ROPE_BASE ** (-jnp.arange(half_width, dtype=jnp.float32) * 2.0 / HEAD_SIZE)
    angles = positions.astype(jnp.float32)[:, None] * frequency[None, :]
    return (jnp.cos(angles), jnp.sin(angles))


def rotate(vector, cosine_rows, sine_rows):
    piece_one, piece_two = jnp.split(vector, 2, axis=-1)
    return jnp.concatenate(
        [
            piece_one * cosine_rows - piece_two * sine_rows,
            piece_two * cosine_rows + piece_one * sine_rows,
        ],
        axis=-1,
    )


def product(left, right):
    return jnp.dot(left, right, preferred_element_type=F32)


def contract_last(left, right):
    return lax.dot_general(left, right, (((1,), (1,)), ((), ())), preferred_element_type=F32)


def token_product(left, right):
    return lax.dot_general(left, right, (((0,), (0,)), ((), ())), preferred_element_type=F32)


def adamw(current, gradient, first, second, step_rate, decay_rate):
    mean_new = BETA_ONE * first + (1.0 - BETA_ONE) * gradient
    square_new = BETA_TWO * second + (1.0 - BETA_TWO) * gradient * gradient
    mean_hat = mean_new / (1.0 - BETA_ONE**STEP)
    square_hat = square_new / (1.0 - BETA_TWO**STEP)
    updated = current - step_rate * (
        mean_hat / (jnp.sqrt(square_hat) + EPS_ADAM) + decay_rate * current
    )
    return (updated, mean_new, square_new)


def pack_heads(weight):
    groups = weight.astype(BF16).reshape(32, 2, 640)
    query = groups[:, :, :512].reshape(32, 2, 2, 256).transpose(1, 2, 0, 3)
    pair = groups[:, :, 512:].transpose(1, 0, 2)[:, None]
    pair = jnp.broadcast_to(pair, (2, 2, 32, 128))
    return jnp.concatenate([query, pair], axis=3).reshape(4, 32, HEADS_COLS)


def unpack_heads(pieces):
    pieces = pieces.astype(F32).reshape(2, 2, 32, HEADS_COLS)
    query = pieces[..., :256].transpose(2, 0, 1, 3).reshape(32, 2, 512)
    pair = (pieces[:, 0, :, 256:] + pieces[:, 1, :, 256:]).transpose(1, 0, 2)
    return jnp.concatenate([query, pair], axis=2).reshape(32, 1280)


def pack_gating(weight):
    cut = weight.astype(BF16).reshape(32, 2, 16, 4, PIECE_USED).transpose(3, 0, 1, 2, 4)
    cut = jnp.pad(cut, ((0, 0),) * 4 + ((0, PIECE - PIECE_USED),))
    return cut.reshape(4, 32, 2 * HIDDEN)


def unpack_gating(pieces):
    cut = pieces.reshape(4, 32, 2, 16, PIECE)[..., :PIECE_USED]
    return cut.transpose(1, 2, 3, 0, 4).reshape(32, 2, 2816).astype(F32)


def pack_down(weight):
    cut = weight.astype(BF16).reshape(4, PIECE_USED, 512)
    return jnp.pad(cut, ((0, 0), (0, PIECE - PIECE_USED), (0, 0)))


def unpack_down(pieces):
    return pieces[:, :PIECE_USED].reshape(4 * PIECE_USED, 512).astype(F32)


def body(
    block_input,
    cotangent,
    norm_gains,
    gains_first,
    gains_second,
    heads_projection_weight,
    heads_first_moment,
    heads_second_moment,
    merge_weight,
    merge_first,
    merge_second,
    gating_weight,
    gating_first,
    gating_second,
    down_weight,
    down_first,
    down_second,
):
    ANY, VMEM = pl.ANY, pltpu.VMEM
    head_scale = HEAD_SIZE ** (-0.5)
    row, col = lax.axis_index("row"), lax.axis_index("col")
    line = col * 4 + row

    def own_rows(values):
        return lax.dynamic_slice_in_dim(values, line * OWN, OWN, axis=0)

    w_heads, gating_own, down_own, w_merge, inputs, gains = call(
        start_kernel,
        [
            (shape(4, 16, 32, HEADS_COLS), ANY),
            (shape(4, 32, 2 * HIDDEN), ANY),
            (shape(PIECE, MODEL_WIDTH), ANY),
            (shape(256, MODEL_WIDTH), ANY),
            (shape(SEQ, MODEL_WIDTH), ANY),
            (shape(4, 8, 128, dtype=F32), ANY),
        ],
        [
            (pack_heads(heads_projection_weight), ANY),
            (pack_gating(gating_weight), ANY),
            (pack_down(down_weight), ANY),
            (merge_weight.astype(BF16), ANY),
            (block_input, ANY),
            (norm_gains.reshape(8, 128), ANY),
        ],
        [],
        100,
        0,
        2**24,
    )
    w_heads = w_heads.reshape(MODEL_WIDTH, HEADS_COLS)
    gains = gains.reshape(4, 2, 512).transpose(1, 0, 2).reshape(2, MODEL_WIDTH)
    input_rows = own_rows(inputs)
    wide = inputs.astype(F32)
    scale_one = lax.rsqrt(jnp.mean(wide * wide, axis=1, keepdims=True) + EPS_NORM)
    normed_one = (wide * scale_one * gains[0]).astype(BF16)

    mixed = product(normed_one, w_heads)
    cosine_rows, sine_rows = rope_tables(jnp.arange(SEQ, dtype=jnp.int32))
    query = rotate(
        mixed[:, :256].reshape(SEQ, 4, HEAD_SIZE), cosine_rows[:, None], sine_rows[:, None]
    ).astype(BF16)
    key = rotate(mixed[:, 256:320], cosine_rows, sine_rows).astype(BF16)
    value = mixed[:, 320:].astype(BF16)
    causal = jnp.arange(SEQ)[:, None] >= jnp.arange(SEQ)[None, :]

    def scores_of():
        raw = jnp.einsum("tqd,sd->qts", query, key, preferred_element_type=F32) * head_scale
        return jnp.where(causal, raw, MASK_FILL)

    scores = scores_of()
    row_max = jnp.max(scores, axis=-1, keepdims=True)
    exponent = jnp.exp(scores - row_max)
    exp_total = jnp.sum(exponent, axis=-1, keepdims=True)
    probs_low = (exponent / exp_total).astype(BF16)
    log_total = row_max + jnp.log(exp_total)
    attended = jnp.einsum("qts,sd->tqd", probs_low, value, preferred_element_type=F32)
    attended = attended.reshape(SEQ, 256).astype(BF16)
    merged = product(attended, w_merge).astype(BF16)

    middle, normed_two, w_gating, w_down, back = call(
        middle_kernel,
        [
            (shape(OWN, MODEL_WIDTH, dtype=F32), VMEM),
            (shape(SEQ, MODEL_WIDTH), ANY),
            (shape(4, 16, 32, 2 * HIDDEN), ANY),
            (shape(16 * PIECE, MODEL_WIDTH), ANY),
            (shape(SEQ, MODEL_WIDTH), ANY),
        ],
        [
            (merged, VMEM),
            (input_rows, VMEM),
            (gains, VMEM),
            (gating_own, ANY),
            (down_own, ANY),
            (cotangent, ANY),
        ],
        LINE_SCATTER_SCRATCH + [pltpu.VMEM((OWN, MODEL_WIDTH), BF16)],
        130,
        1,
        2**25,
    )
    w_gating = w_gating.reshape(MODEL_WIDTH, 2 * HIDDEN)

    gated = product(normed_two, w_gating)
    gate_value, up_value = gated[:, :HIDDEN], gated[:, HIDDEN:]
    gate_sigmoid = jax.nn.sigmoid(gate_value)
    silu_gate = gate_value * gate_sigmoid
    hidden = (silu_gate * up_value).astype(BF16)
    grad_hidden = contract_last(back, w_down)
    grad_gate = grad_hidden * up_value * gate_sigmoid * (1.0 + gate_value * (1.0 - gate_sigmoid))
    grad_up = grad_hidden * silu_gate
    grad_gated = jnp.concatenate([grad_gate, grad_up], axis=1).astype(BF16)
    down_out = product(hidden, w_down).astype(BF16)
    down_part = token_product(hidden, back).astype(BF16)
    gating_part = token_product(normed_two, grad_gated).astype(BF16)
    normed_two_part = contract_last(grad_gated, w_gating).astype(BF16)

    grad_middle, branch, gain_part, gating_sum, down_sum = call(
        branch_kernel,
        [
            (shape(OWN, MODEL_WIDTH, dtype=F32), VMEM),
            (shape(SEQ, MODEL_WIDTH), ANY),
            (shape(8, MODEL_WIDTH, dtype=F32), VMEM),
            (shape(4, 32, 2 * HIDDEN), VMEM),
            (shape(PIECE, MODEL_WIDTH), VMEM),
        ],
        [
            (normed_two_part, VMEM),
            (middle, VMEM),
            (own_rows(back), VMEM),
            (gains, VMEM),
            (gating_part.reshape(4, 16, 32, 2 * HIDDEN), VMEM),
            (down_part, VMEM),
        ],
        LINE_SCATTER_SCRATCH
        + ring_scatter_scratch(Rows(2 * HIDDEN))
        + ring_scatter_scratch(Flat())
        + [pltpu.VMEM((OWN, MODEL_WIDTH), BF16)],
        130,
        2,
        2**25,
    )

    merge_part = token_product(attended, branch).astype(BF16)
    grad_attended = contract_last(branch, w_merge).astype(BF16).reshape(SEQ, 4, HEAD_SIZE)
    soft = jnp.exp(scores_of() - log_total)
    grad_probs = jnp.einsum("tqd,sd->qts", grad_attended, value, preferred_element_type=F32)
    inner_sum = jnp.sum(soft * grad_probs, axis=-1, keepdims=True)
    grad_scores = (soft * (grad_probs - inner_sum)).astype(BF16)
    grad_query = (
        jnp.einsum("qts,sd->tqd", grad_scores, key, preferred_element_type=F32) * head_scale
    )
    grad_key = (
        jnp.einsum("qts,tqd->sd", grad_scores, query, preferred_element_type=F32) * head_scale
    )
    grad_value = jnp.einsum(
        "qts,tqd->sd", soft.astype(BF16), grad_attended, preferred_element_type=F32
    )
    grad_query = rotate(grad_query, cosine_rows[:, None], -sine_rows[:, None]).reshape(SEQ, 256)
    grad_key = rotate(grad_key, cosine_rows, -sine_rows)
    grad_mixed = jnp.concatenate([grad_query, grad_key, grad_value], axis=1).astype(BF16)
    heads_part = token_product(normed_one, grad_mixed).astype(BF16)
    normed_one_part = contract_last(grad_mixed, w_heads).astype(BF16)

    (
        block_output, input_grad, gains_grad,
        heads_pieces, merge_pieces, gating_pieces, down_pieces,
    ) = call(
        finish_kernel,
        [
            (shape(512, 512), ANY),
            (shape(512, 512, dtype=F32), ANY),
            (shape(8, 512, dtype=F32), VMEM),
            (shape(4, 32, HEADS_COLS), ANY),
            (shape(16, 64, 512), ANY),
            (shape(4, 32, 2 * HIDDEN), ANY),
            (shape(4, PIECE, 512), ANY),
        ],
        [
            (normed_one_part, VMEM),
            (down_out, VMEM),
            (middle, VMEM),
            (grad_middle, VMEM),
            (input_rows, VMEM),
            (gains, VMEM),
            (gain_part, VMEM),
            (heads_part.reshape(4, 16, 32, HEADS_COLS), VMEM),
            (merge_part, ANY),
            (gating_sum, ANY),
            (down_sum, ANY),
        ],
        LINE_SCATTER_SCRATCH
        + LINE_SCATTER_SCRATCH
        + ring_scatter_scratch(Rows(HEADS_COLS))
        + [
            pltpu.VMEM((4, 32, HEADS_COLS), BF16),
            pltpu.VMEM((OWN, MODEL_WIDTH), BF16),
            pltpu.VMEM((OWN, MODEL_WIDTH), F32),
            pltpu.VMEM((2, 8, MODEL_WIDTH), F32),
            pltpu.VMEM((4, 2, 8, 512), F32),
            pltpu.VMEM((32, 8, 512), F32),
        ],
        180,
        3,
        2**25,
    )
    gains_grad = gains_grad[:2]
    heads_grad = unpack_heads(heads_pieces)
    merge_grad = jnp.sum(merge_pieces.astype(F32), axis=0)
    gating_grad = unpack_gating(gating_pieces)
    down_grad = unpack_down(down_pieces)
    gains_next, gains_mean, gains_square = adamw(
        norm_gains, gains_grad, gains_first, gains_second, RATE_GAIN, 0.0
    )
    heads_next, heads_mean, heads_square = adamw(
        heads_projection_weight,
        heads_grad,
        heads_first_moment,
        heads_second_moment,
        RATE_MATRIX,
        WEIGHT_DECAY,
    )
    merge_next, merge_mean, merge_square = adamw(
        merge_weight, merge_grad, merge_first, merge_second, RATE_MERGE, WEIGHT_DECAY
    )
    gating_next, gating_mean, gating_square = adamw(
        gating_weight, gating_grad, gating_first, gating_second, RATE_MATRIX, WEIGHT_DECAY
    )
    down_next, down_mean, down_square = adamw(
        down_weight, down_grad, down_first, down_second, RATE_MATRIX, WEIGHT_DECAY
    )
    return (
        block_output,
        input_grad,
        gains_grad,
        gains_next,
        gains_mean,
        gains_square,
        heads_grad,
        heads_next,
        heads_mean,
        heads_square,
        merge_grad,
        merge_next,
        merge_mean,
        merge_square,
        gating_grad,
        gating_next,
        gating_mean,
        gating_square,
        down_grad,
        down_next,
        down_mean,
        down_square,
    )


def solution(mesh):
    in_specs = (
        P(("dp", "col"), "row"),
        P(("dp", "col"), "row"),
        P(None, "row"),
        P(None, "row"),
        P(None, "row"),
        P(("row", "dp"), "col"),
        P(("row", "dp"), "col"),
        P(("row", "dp"), "col"),
        P(("col", "dp"), "row"),
        P(("col", "dp"), "row"),
        P(("col", "dp"), "row"),
        P(("row", "dp"), None, "col"),
        P(("row", "dp"), None, "col"),
        P(("row", "dp"), None, "col"),
        P(("col", "dp"), "row"),
        P(("col", "dp"), "row"),
        P(("col", "dp"), "row"),
    )
    out_specs = (
        P(("dp", "col"), "row"),
        P(("dp", "col"), "row"),
        P(None, "row"),
        P(None, "row"),
        P(None, "row"),
        P(None, "row"),
        P(("row", "dp"), "col"),
        P(("row", "dp"), "col"),
        P(("row", "dp"), "col"),
        P(("row", "dp"), "col"),
        P(("col", "dp"), "row"),
        P(("col", "dp"), "row"),
        P(("col", "dp"), "row"),
        P(("col", "dp"), "row"),
        P(("row", "dp"), None, "col"),
        P(("row", "dp"), None, "col"),
        P(("row", "dp"), None, "col"),
        P(("row", "dp"), None, "col"),
        P(("col", "dp"), "row"),
        P(("col", "dp"), "row"),
        P(("col", "dp"), "row"),
        P(("col", "dp"), "row"),
    )
    return jax.shard_map(body, mesh=mesh, in_specs=in_specs, out_specs=out_specs, check_vma=False)
```

time: 1640 us -> 510 us (0.31)
  the two profiles are of different devices: /device:TPU:0 before, /device:TPU:25 now
where the time goes in v1:
time: 510 us; the launch traced here: 502 us
  Pallas kernels  336 us (66%)
  matrix products  101 us (20%)
  other arithmetic  40 us (8%)
  local copies, waits for them, and re-layouts  23.2 us (5%)
    pallas_call x4, Pallas kernels, call(): pl.pallas_call(kernel, out_shape=[shape for shape, _ in outs], in_specs=[...  336 us
    dot_general x4, matrix products, product(): return jnp.dot(left, right, preferred_element_type=F32)  22.5 us
    dot_general x4, matrix products, contract_last(): lax.dot_general(left, right, (((1,), (1,)), ((), ())), preferred_element_...  22.1 us
    dot_general x4, matrix products, token_product(): lax.dot_general(left, right, (((0,), (0,)), ((), ())), preferred_element_...  20.5 us
    sub x5, other arithmetic, adamw(): current - step_rate * (mean_hat / (jnp.sqrt(square_hat) + EPS_ADAM) + dec...  10.4 us

profile of v1, /device:TPU:25, one launch (start us, length us, event | category | flops | bytes accessed | tf_op | source)
XLA Modules:
  0.0 501.7 jit_solution(9446631651604684092)
XLA Ops:
  0.7 1.3 reshape.226.gains_own
  2.0 1.5 convert_element_type.134.merge_own
  3.5 0.9 convert_element_type.131
  5.5 1.0 convert_element_type.133
  7.2 1.4 convert_element_type.132
  8.6 3.1 reshape.223
  12.1 2.8 reshape.224.gating_own
  15.2 64.5 %shard_map.336 = (bf16[4,16,32,384]{3,2,1,0:T(8,128)(2,1)}, bf16[4,32,1536]{2,1,0:T(8,128)(2,1)}, bf16[48,2048]{1,0:T(8,128)(2,1)}, bf16[256,2048]{1,0:T(8,128)(...) custom-call(bf16[4,32,384]{2,1,0:T(8,128)(2,1)} %bitcast.129, bf16[4,32,1536]{2,1,0:T(8,128)(2,1)} %reshape.224.gating_own, ...), custom_call_target="tpu_custom_call" | custom-call | bytes 16777216 | tf_op jit(solution)/shard_map/pallas_call | solution.py:428
  80.4 3.2 fusion.5
  84.3 0.8 constant_dynamic-slice_fusion.1.input_rows
  85.2 3.5 fusion.16
  89.5 7.5 %fusion.63 = (f32[4,1024]{1,0:T(4,128)S(1)}, f32[4,1024,1024]{1,2,0:T(8,128)}) fusion(bf16[1024,4,32]{0,2,1:T(8,128)(2,1)S(1)} %get-tuple-element.92, bf16[1024,4,32]{0,2,1:T(8,128)(2,1)S(1)} %get-tuple-element.91, bf16[1024,32]{0,1:T(8,128)(2,1)S(1)} %get-tuple-element.99, bf16[1024,32]{0,1:T(8,128)(2,1)S(1)} %get-tuple-element.100, ...), kind=kOutput, calls=%fused_computation.120 | convolution fusion | flops 550760448 | bytes 18497536 | tf_op jit(solution)/shard_map/tqd,sd->qts/dot_general | solution.py:1061
  97.0 8.0 %fusion.3 = f32[4,1024]{1,0:T(4,128)S(1)} fusion(f32[4,1024,1024]{1,2,0:T(8,128)} %get-tuple-element.103, f32[4,1024]{1,0:T(4,128)S(1)} %get-tuple-element.102), kind=kLoop, calls=%fused_computation.9 | loop fusion | flops 8384512 | bytes 16809984 | tf_op jit(solution)/shard_map/reduce_sum | solution.py:1067
  105.1 7.5 %fusion.14 = bf16[64,4,1024]{2,0,1:T(8,128)(2,1)S(1)} fusion(f32[4,1024,1024]{1,2,0:T(8,128)} %get-tuple-element.103, f32[4,1024]{1,0:T(4,128)S(1)} %fusion.3, f32[4,1024]{1,0:T(4,128)S(1)} %get-tuple-element.102, f32[1024,384]{0,1:T(8,128)S(1)} %fusion.16), kind=kOutput, calls=%fused_computation.39 | convolution fusion | flops 549715968 | bytes 17465344 | tf_op jit(solution)/shard_map/qts,sd->tqd/dot_general | solution.py:1070
  112.6 3.3 convolution_convert_fusion.3.part
  115.9 103.9 %shard_map.337 = (f32[128,2048]{1,0:T(8,128)}, bf16[1024,2048]{1,0:T(8,128)(2,1)}, bf16[4,16,32,1536]{3,2,1,0:T(8,128)(2,1)}, bf16[768,2048]{1,0:T(8,128)(2,1)}, bf16[1024,2048]{1,0:T(8,128)(2,1)}) custom-call(bf16[1024,2048]{1,0:T(8,128)(2,1)} %convolution_convert_fusion.3.part, bf16[128,2048]{1,0:T(8,128)(2,1)} %constant_dynamic-slice_fusion.1.input_rows, ...), custom_call_target="tpu_custom_call" | custom-call | bytes 33554432 | tf_op jit(solution)/shard_map/pallas_call | solution.py:428
  219.8 1.9 constant_dynamic-slice_fusion.back_rows
  221.7 10.7 %fusion.64 = f32[1024,1536]{0,1:T(8,128)S(1)} fusion(bf16[1024,2048]{1,0:T(8,128)(2,1)} %get-tuple-element.53, bf16[2048,1536]{1,0:T(8,128)(2,1)} %bitcast.139), kind=kOutput, calls=%fused_computation.121 | convolution fusion | flops 6442450944 | bytes 16777216 | tf_op jit(solution)/shard_map/dot_general | solution.py:937
  232.4 5.9 %multiply_convert_fusion.2 = (bf16[1024,768]{0,1:T(8,128)(2,1)}, bf16[1024,768]{0,1:T(8,128)(2,1)}, bf16[1024,768]{0,1:T(8,128)(2,1)S(1)}) fusion(f32[1024,1536]{0,1:T(8,128)S(1)} %fusion.64, bf16[1024,2048]{1,0:T(8,128)(2,1)S(1)} %copy-done.16, bf16[768,2048]{1,0:T(8,128)(2,1)S(1)} %copy-done.22), kind=kOutput, calls=%fused_computation.29 | convolution fusion | flops 3233021952 | bytes 18350080 | tf_op jit(solution)/shard_map/dot_general | solution.py:941
  238.4 4.8 convolution_convert_fusion.5.down_part
  243.2 8.3 %convolution_convert_fusion.1.part = bf16[1024,2048]{1,0:T(8,128)(2,1)} fusion(bf16[2048,1536]{1,0:T(8,128)(2,1)S(1)} %bitcast.142, bf16[1024,768]{0,1:T(8,128)(2,1)S(1)} %copy-done.28, bf16[1024,768]{0,1:T(8,128)(2,1)S(1)} %copy-done.27), kind=kOutput, calls=%fused_computation.21 | convolution fusion | flops 6450839552 | bytes 13631488 | tf_op jit(solution)/shard_map/dot_general | solution.py:941
  251.5 9.5 %convolution_convert_fusion = bf16[2048,1536]{1,0:T(8,128)(2,1)} fusion(bf16[1024,2048]{1,0:T(8,128)(2,1)S(1)} %copy-done.20, bf16[1024,768]{0,1:T(8,128)(2,1)S(1)} %copy-done.28, bf16[1024,768]{0,1:T(8,128)(2,1)S(1)} %copy-done.27), kind=kOutput, calls=%fused_computation.19 | convolution fusion | flops 6451888128 | bytes 13631488 | tf_op jit(solution)/shard_map/dot_general | solution.py:945
  261.0 65.5 %shard_map.338 = (f32[128,2048]{1,0:T(8,128)}, bf16[1024,2048]{1,0:T(8,128)(2,1)}, f32[8,2048]{1,0:T(8,128)}, bf16[4,32,1536]{2,1,0:T(8,128)(2,1)}, bf16[48,2048]{1,0:T(8,128)(2,1)}) custom-call(bf16[1024,2048]{1,0:T(8,128)(2,1)} %convolution_convert_fusion.1.part, f32[128,2048]{1,0:T(8,128)} %get-tuple-element.55.middle, ...), custom_call_target="tpu_custom_call" | custom-call | bytes 33554432 | tf_op jit(solution)/shard_map/pallas_call | solution.py:428
  326.5 3.5 convolution_convert_fusion.8
  330.0 8.6 %fusion.22 = bf16[1024,64]{0,1:T(8,128)(2,1)S(1)} fusion(bf16[1024,4,64]{0,2,1:T(8,128)(2,1)S(1)} %bitcast.117, f32[4,1024,1024]{1,2,0:T(8,128)} %get-tuple-element.103, f32[4,1024]{1,0:T(4,128)S(1)} %log_add_fusion), kind=kOutput, calls=%fused_computation.44 | convolution fusion | flops 545325056 | bytes 17448960 | tf_op jit(solution)/shard_map/qts,tqd->sd/dot_general | solution.py:1150
  338.7 2.3 convolution_convert_fusion.7.merge_part
  340.9 5.1 %convolution_convert_fusion.4.down_out = bf16[1024,2048]{1,0:T(8,128)(2,1)} fusion(bf16[1024,768]{0,1:T(8,128)(2,1)S(1)} %copy-done.26, bf16[768,2048]{1,0:T(8,128)(2,1)S(1)} %copy-done.23), kind=kOutput, calls=%fused_computation.24 | convolution fusion | flops 3223322624 | bytes 8912896 | tf_op jit(solution)/shard_map/dot_general | solution.py:937
  346.1 7.5 %fusion = (f32[4,1024]{1,0:T(4,128)S(1)}, f32[1024,1024,4]{1,0,2:T(8,128)}) fusion(f32[4,1024,1024]{1,2,0:T(8,128)S(1)} %bitcast.113, f32[4,1024]{1,0:T(4,128)S(1)} %log_add_fusion, bf16[1024,4,64]{0,2,1:T(8,128)(2,1)S(1)} %bitcast.118, f32[1024,384]{0,1:T(8,128)S(1)} %fusion.16), kind=kOutput, calls=%fused_computation.2 | convolution fusion | flops 549449728 | bytes 34242560 | tf_op jit(solution)/shard_map/tqd,sd->qts/dot_general | solution.py:1141
  353.6 8.0 %fusion.2 = bf16[4,1024,1024]{1,2,0:T(8,128)(2,1)S(1)} fusion(f32[1024,1024,4]{1,0,2:T(8,128)} %get-tuple-element.105, f32[4,1024,1024]{1,2,0:T(8,128)S(1)} %bitcast.113, f32[4,1024]{1,0:T(4,128)S(1)} %get-tuple-element.104, f32[4,1024]{1,0:T(4,128)S(1)} %log_add_fusion), kind=kLoop, calls=%fused_computation.4 | loop fusion | flops 16777216 | bytes 41975808 | tf_op jit(solution)/shard_map/convert_element_type | solution.py:1143
  361.6 2.7 fusion.18
  364.3 1.6 fusion.13
  366.6 3.9 convolution_convert_fusion.6
  370.6 4.4 convolution_convert_fusion.2.part
  375.0 102.2 %shard_map.339 = (bf16[512,512]{1,0:T(8,128)(2,1)}, f32[512,512]{1,0:T(8,128)}, f32[8,512]{1,0:T(8,128)}, bf16[4,32,384]{2,1,0:T(8,128)(2,1)}, bf16[16,64,512]{2...) custom-call(bf16[1024,2048]{1,0:T(8,128)(2,1)} %convolution_convert_fusion.2.part, ...), custom_call_target="tpu_custom_call" | custom-call | bytes 33554432 | tf_op jit(solution)/shard_map/pallas_call | solution.py:428
  477.2 1.5 add_subtract_fusion
  478.7 1.4 convert_reduce_fusion
  480.1 0.9 slice.64
  481.3 0.9 convert.54
  482.2 1.0 slice_convert_fusion.1
  484.0 0.8 multiply_subtract_fusion.3
  484.9 0.8 multiply_subtract_fusion.2
  485.7 1.1 reshape.240
  487.1 1.8 copy.80
  488.9 3.3 reshape.243
  492.2 2.8 multiply_subtract_fusion.1
  494.9 4.6 multiply_subtract_fusion
  499.5 0.8 copy.108
  500.3 1.0 copy.109
  (108 shorter events, 6.8 us)
Async XLA Ops:
  80.4 3.9 copy-start
  105.0 7.5 %copy-start.5 = (bf16[256,2048]{1,0:T(8,128)(2,1)S(1)}, bf16[256,2048]{1,0:T(8,128)(2,1)}, u32[]{:S(2)}) copy-start(bf16[256,2048]{1,0:T(8,128)(2,1)} %get-tuple-element.48) | copy-start | bytes 3145732
  221.7 10.7 %copy-start.16 = (bf16[1024,2048]{1,0:T(8,128)(2,1)S(1)}, bf16[1024,2048]{1,0:T(8,128)(2,1)}, u32[]{:S(2)}) copy-start(bf16[1024,2048]{1,0:T(8,128)(2,1)} %get-tuple-element.51) | copy-start | bytes 12582916
  221.7 10.7 %copy-start.22 = (bf16[768,2048]{1,0:T(8,128)(2,1)S(1)}, bf16[768,2048]{1,0:T(8,128)(2,1)}, u32[]{:S(2)}) copy-start(bf16[768,2048]{1,0:T(8,128)(2,1)} %get-tuple-element.52) | copy-start | bytes 9437188
  221.7 21.4 %slice-start.4 = ((s8[6291456]{0:T(1024)(128)(4,1)}), s8[4194304]{0:T(1024)(128)(4,1)S(1)}, s32[]{:S(2)}) async-start(s8[6291456]{0:T(1024)(128)(4,1)} %bitcast.140), calls=%async_computation.4 | async-start | bytes 8388608
  232.4 10.7 %slice-start.5 = ((s8[6291456]{0:T(1024)(128)(4,1)}), s8[2097152]{0:T(1024)(128)(4,1)S(1)}, s32[]{:S(2)}) async-start(s8[6291456]{0:T(1024)(128)(4,1)} %bitcast.140), calls=%async_computation.5 | async-start | bytes 4194304
  238.4 4.8 copy-start.25
  238.4 4.8 copy-start.27
  238.4 4.8 copy-start.28
  243.2 8.3 %copy-start.20 = (bf16[1024,2048]{1,0:T(8,128)(2,1)S(1)}, bf16[1024,2048]{1,0:T(8,128)(2,1)}, u32[]{:S(2)}) copy-start(bf16[1024,2048]{1,0:T(8,128)(2,1)} %get-tuple-element.53) | copy-start | bytes 12582916
  330.0 8.6 %copy-start.21 = (bf16[1024,2048]{1,0:T(8,128)(2,1)S(1)}, bf16[1024,2048]{1,0:T(8,128)(2,1)}, u32[]{:S(2)}) copy-start(bf16[1024,2048]{1,0:T(8,128)(2,1)} %get-tuple-element.56) | copy-start | bytes 12582916
  330.0 10.9 %copy-start.23 = (bf16[768,2048]{1,0:T(8,128)(2,1)S(1)}, bf16[768,2048]{1,0:T(8,128)(2,1)}, u32[]{:S(2)}) copy-start(bf16[768,2048]{1,0:T(8,128)(2,1)} %get-tuple-element.52) | copy-start | bytes 9437188
  330.0 16.0 %slice-start = ((s8[16777216]{0:T(1024)(128)(4,1)}), s8[4194304]{0:T(1024)(128)(4,1)S(1)}, s32[]{:S(2)}) async-start(s8[16777216]{0:T(1024)(128)(4,1)} %bitcast.112), calls=%async_computation | async-start | bytes 8388608
  330.0 16.0 %slice-start.1 = ((s8[16777216]{0:T(1024)(128)(4,1)}), s8[4194304]{0:T(1024)(128)(4,1)S(1)}, s32[]{:S(2)}) async-start(s8[16777216]{0:T(1024)(128)(4,1)} %bitcast.112), calls=%async_computation.1 | async-start | bytes 8388608
  338.7 2.3 copy-start.26
  338.7 7.4 %slice-start.2 = ((s8[16777216]{0:T(1024)(128)(4,1)}), s8[4194304]{0:T(1024)(128)(4,1)S(1)}, s32[]{:S(2)}) async-start(s8[16777216]{0:T(1024)(128)(4,1)} %bitcast.112), calls=%async_computation.2 | async-start | bytes 8388608
  340.9 5.1 %slice-start.3 = ((s8[16777216]{0:T(1024)(128)(4,1)}), s8[4194304]{0:T(1024)(128)(4,1)S(1)}, s32[]{:S(2)}) async-start(s8[16777216]{0:T(1024)(128)(4,1)} %bitcast.112), calls=%async_computation.3 | async-start | bytes 8388608
  364.3 2.4 copy-start.1
  366.6 4.0 copy-start.24
  375.0 102.2 %copy-start.17 = (f32[2,512]{1,0:T(2,128)S(1)}, f32[2,512]{1,0:T(2,128)}, u32[]{:S(2)}) copy-start(f32[2,512]{1,0:T(2,128)} %param.19) | copy-start | bytes 12292
  375.0 102.3 %copy-start.18 = (f32[2,512]{1,0:T(2,128)S(1)}, f32[2,512]{1,0:T(2,128)}, u32[]{:S(2)}) copy-start(f32[2,512]{1,0:T(2,128)} %param.20) | copy-start | bytes 12292
  375.0 102.3 %copy-start.19 = (f32[2,512]{1,0:T(2,128)S(1)}, f32[2,512]{1,0:T(2,128)}, u32[]{:S(2)}) copy-start(f32[2,512]{1,0:T(2,128)} %param.21) | copy-start | bytes 12292
  477.1 6.9 %copy-start.9 = (f32[64,512]{1,0:T(8,128)S(1)}, f32[64,512]{1,0:T(8,128)}, u32[]{:S(2)}) copy-start(f32[64,512]{1,0:T(8,128)} %param.25) | copy-start | bytes 393220
  477.1 6.9 %copy-start.14 = (f32[64,512]{1,0:T(8,128)S(1)}, f32[64,512]{1,0:T(8,128)}, u32[]{:S(2)}) copy-start(f32[64,512]{1,0:T(8,128)} %param.26) | copy-start | bytes 393220
  477.1 6.9 %copy-start.15 = (f32[64,512]{1,0:T(8,128)S(1)}, f32[64,512]{1,0:T(8,128)}, u32[]{:S(2)}) copy-start(f32[64,512]{1,0:T(8,128)} %param.27) | copy-start | bytes 393220
  477.2 7.7 %copy-start.7 = (f32[32,1280]{1,0:T(8,128)S(1)}, f32[32,1280]{1,0:T(8,128)}, u32[]{:S(2)}) copy-start(f32[32,1280]{1,0:T(8,128)} %param.22) | copy-start | bytes 491524
  477.2 7.7 %copy-start.12 = (f32[32,1280]{1,0:T(8,128)S(1)}, f32[32,1280]{1,0:T(8,128)}, u32[]{:S(2)}) copy-start(f32[32,1280]{1,0:T(8,128)} %param.23) | copy-start | bytes 491524
  477.2 7.7 %copy-start.13 = (f32[32,1280]{1,0:T(8,128)S(1)}, f32[32,1280]{1,0:T(8,128)}, u32[]{:S(2)}) copy-start(f32[32,1280]{1,0:T(8,128)} %param.24) | copy-start | bytes 491524
  477.2 8.5 %copy-start.11 = (bf16[4,32,1536]{2,1,0:T(8,128)(2,1)S(1)}, bf16[4,32,1536]{2,1,0:T(8,128)(2,1)}, u32[]{:S(2)}) copy-start(bf16[4,32,1536]{2,1,0:T(8,128)(2,1)} %get-tuple-element.66) | copy-start | bytes 1179652
  480.1 5.6 %copy-start.8 = (f32[64,512]{1,0:T(8,128)}, f32[64,512]{1,0:T(8,128)S(1)}, u32[]{:S(2)}) copy-start(f32[64,512]{1,0:T(8,128)S(1)} %convert_reduce_fusion) | copy-start | bytes 393220
  482.2 3.5 copy-start.6
  487.1 7.9 %copy-start.2 = (f32[32,2,2816]{2,1,0:T(2,128)S(1)}, f32[32,2,2816]{2,1,0:T(2,128)}, u32[]{:S(2)}) copy-start(f32[32,2,2816]{2,1,0:T(2,128)} %param.28) | copy-start | bytes 2162692
  492.2 8.1 %copy-start.3 = (f32[32,2,2816]{2,1,0:T(2,128)}, f32[32,2,2816]{2,1,0:T(2,128)S(1)}, u32[]{:S(2)}) copy-start(f32[32,2,2816]{2,1,0:T(2,128)S(1)} %reshape.243) | copy-start | bytes 2162692
  492.2 7.3 %copy-start.10 = (bf16[512,512]{1,0:T(8,128)(2,1)S(1)}, bf16[512,512]{1,0:T(8,128)(2,1)}, u32[]{:S(2)}) copy-start(bf16[512,512]{1,0:T(8,128)(2,1)} %get-tuple-element.128) | copy-start | bytes 1572868
  492.2 8.1 %copy-start.4 = (f32[512,512]{1,0:T(8,128)S(1)}, f32[512,512]{1,0:T(8,128)}, u32[]{:S(2)}) copy-start(f32[512,512]{1,0:T(8,128)} %get-tuple-element.129) | copy-start | bytes 3145732

commit v2 on v1

--- a/solution.py
+++ b/solution.py
@@ -448,138 +448,176 @@
 
 
 def merge_devices(place):
+    users = [{"dp": j * 4 + place.z, "row": place.y, "col": place.col} for j in range(4)]
     homes = [
-        {"dp": place.row * 4 + z, "row": jnp.int32(row), "col": place.col}
-        for z in range(4)
-        for row in range(4)
+        {"dp": place.row * 4 + place.z, "row": jnp.int32(row), "col": place.col} for row in range(4)
     ]
-    users = [{"dp": jnp.int32(dp), "row": place.y, "col": place.col} for dp in range(16)]
-    return homes, users
+    return users, homes
+
+
+def signal_others(place, devices):
+    barrier = pltpu.get_barrier_semaphore()
+    for device in devices:
+        alone = (device["dp"] == place.dp) & (device["row"] == place.row)
+
+        @pl.when(jnp.logical_not(alone))
+        def _():
+            pl.semaphore_signal(barrier, inc=1, device_id=device, device_id_type=MESH)
+
+
+def merge_exchange(place, wires, devices, source, target, mine):
+    base = wires.count
+    wires.count += 4
+    copies = []
+    for index, device in enumerate(devices):
+        copy = pltpu.make_async_remote_copy(
+            src_ref=source(index),
+            dst_ref=target(index),
+            send_sem=wires.send.at[base + index],
+            recv_sem=wires.recv.at[base + mine],
+            device_id=device,
+            device_id_type=MESH,
+        )
+        here = pltpu.make_async_copy(source(index), target(index), wires.recv.at[base + mine])
+        alone = (device["dp"] == place.dp) & (device["row"] == place.row)
+        copies.append((copy, alone))
+        pl.when(alone)(here.start)
+        pl.when(jnp.logical_not(alone))(copy.start)
+
+    def wait():
+        for index in range(4):
+            pltpu.make_async_copy(source(0), target(0), wires.recv.at[base + index]).wait()
+        for copy, alone in copies:
+            pl.when(jnp.logical_not(alone))(copy.wait_send)
+
+    return wait
+
+
+def nested(plans):
+    pending = [[next(plan), order, plan] for order, plan in enumerate(plans)]
+    while pending:
+        pending.sort(key=lambda entry: entry[:2])
+        entry = pending[0]
+        yield entry[0]
+        try:
+            entry[0] = max(entry[0], next(entry[2]))
+        except StopIteration:
+            pending.pop(0)
+
+
+def column_block(ref, row):
+    return ref.at[:, pl.ds(pl.multiple_of(row * 512, 512), 512)]
+
+
+def down_slot(ref, slot, row):
+    rows = pl.ds(pl.multiple_of(slot * PIECE, PIECE), PIECE)
+    return ref.at[rows, pl.ds(pl.multiple_of(row * 512, 512), 512)]
 
 
 def start_kernel(
-    heads_own, gating_own, down_own, merge_own, input_own, gains_own,
-    heads, gating, down, merge, inputs, gains,
-    send, recv, local,
+    heads_weight, merge_weight, gating_weight, down_weight, input_own, back_own, gains_own,
+    heads, gating, down, inputs, back, gains,
+    heads_cut, merge_cut, gating_cut, down_cut, send, recv, local,
 ):
     place = Place()
     wires = Wires(send, recv, local)
-    homes, users = merge_devices(place)
+    users, homes = merge_devices(place)
     peers = [place.peer(step) for step in (1, 2, 3)]
     same = place.row == place.y
-    barrier = pltpu.get_barrier_semaphore()
     devices = ring_neighbours(place) + line_neighbours(place) + [p for _, p in peers]
-    for device in devices:
-        pl.semaphore_signal(barrier, inc=1, device_id=device, device_id_type=MESH)
-    for index, device in enumerate(homes):
-        alone = (device["dp"] == place.dp) & (device["row"] == place.row)
-
-        @pl.when(jnp.logical_not(alone))
-        def _():
-            pl.semaphore_signal(barrier, inc=1, device_id=device, device_id_type=MESH)
-
-    pl.semaphore_wait(barrier, len(devices) + 16 - same.astype(jnp.int32))
-
-    def down_columns(ref, row):
-        return ref.at[:, pl.ds(pl.multiple_of(row * 512, 512), 512)]
+    signal_others(place, devices + homes)
+    pl.semaphore_wait(
+        pltpu.get_barrier_semaphore(), len(devices) + 4 - same.astype(jnp.int32)
+    )
 
     def exchange():
-        yield 0.0
-        moved = []
-        kept = wires.keep(heads_own.at[place.row], heads.at[place.row, place.dp])
-        for other, device in peers:
-            moved.append(
-                wires.push(heads_own.at[other], heads.at[place.row, place.dp], device)
-            )
+        yield 0.2
+        for row in range(4):
+            group, half = divmod(row, 2)
+            query = heads_weight[:, pl.ds(group * 640 + half * 256, 256)]
+            heads_cut[row, :, pl.ds(0, 256)] = query.astype(BF16)
+            pair = heads_weight[:, pl.ds(group * 640 + 512, 128)]
+            heads_cut[row, :, pl.ds(256, 128)] = pair.astype(BF16)
+            for side in range(2):
+                piece = merge_weight[pl.ds(16 * row, 16), pl.ds(256 * side, 256)]
+                merge_cut[row, pl.ds(16 * side, 16)] = piece.astype(BF16)
+
+        def heads_columns(row, slot):
+            return heads.at[row, slot, :, pl.ds(0, HEADS_COLS)]
+
+        moved = [
+            wires.push(heads_cut.at[other], heads_columns(place.row, place.dp), device)
+            for other, device in peers
+        ]
+        kept = [wires.keep(heads_cut.at[place.row], heads_columns(place.row, place.dp))]
+        merge_wait = merge_exchange(
+            place, wires, users,
+            lambda j: merge_cut.at[j],
+            lambda j: heads.at[place.row, j * 4 + place.z, :, pl.ds(HEADS_COLS, 256)],
+            place.row,
+        )
         for other, device in peers:
             moved.append(wires.push(gains_own, gains.at[place.row], device))
-        kept_gains = wires.keep(gains_own, gains.at[place.row])
-        yield 0.2
-        rest = [
-            wires.keep(gating_own.at[place.row], gating.at[place.row]),
-            wires.keep(down_own.at[place.row], down_columns(down, place.row)),
+        kept.append(wires.keep(gains_own, gains.at[place.row]))
+        for row in range(4):
+            piece = down_weight[pl.ds(PIECE_USED * row, PIECE_USED), :]
+            down_cut[row] = jnp.concatenate(
+                [piece, jnp.zeros((PIECE - PIECE_USED, 512), F32)], axis=0
+            ).astype(BF16)
+        later = [
+            wires.push(down_cut.at[other], down_slot(down, place.dp, place.row), device)
+            for other, device in peers
         ]
-        later = []
-        for other, device in peers:
-            later.append(wires.push(gating_own.at[other], gating.at[place.row], device))
-            later.append(
-                wires.push(down_own.at[other], down_columns(down, place.row), device)
-            )
-        yield 4.0
-        kept.wait()
-        kept_gains.wait()
+        kept.append(wires.keep(down_cut.at[place.row], down_slot(down, place.dp, place.row)))
+        yield 5.0
+        for copy in kept:
+            copy.wait()
         for copy in moved:
             copy.wait_recv()
-        sides = [
-            ring_gather(place, wires, Rows(HEADS_COLS), heads, side, 4.1, 1.1) for side in (0, 1)
+        merge_wait()
+        plans = [
+            ring_gather(place, wires, Rows(HEADS_COLS + 256), heads, side, 5.0, 1.8)
+            for side in (0, 1)
         ]
-        pending = [(next(plan), plan) for plan in sides]
-        while pending:
-            pending.sort(key=lambda entry: entry[0])
-            when, plan = pending[0]
-            yield when
-            try:
-                pending[0] = (next(plan), plan)
-            except StopIteration:
-                pending.pop(0)
-        yield 30.0
-        for copy in rest:
-            copy.wait()
         for copy in later:
             copy.wait_recv()
-
-    def merge_rows():
-        yield 0.15
-        target = merge.at[
-            pl.ds(pl.multiple_of(place.z * 64, 64), 64),
-            pl.ds(pl.multiple_of(place.row * 512, 512), 512),
+        plans += [ring_gather(place, wires, Flat(), down, side, 7.0, 4.0) for side in (0, 1)]
+        yield from nested(plans)
+
+    def gating_exchange():
+        yield 5.5
+        zeros = jnp.zeros((32, PIECE - PIECE_USED), F32)
+        for kind in range(2):
+            for row in range(4):
+                pieces = []
+                for slot in range(16):
+                    first = slot * 4 * PIECE_USED + row * PIECE_USED
+                    pieces += [gating_weight[:, kind, pl.ds(first, PIECE_USED)], zeros]
+                gating_cut[row, :, pl.ds(kind * HIDDEN, HIDDEN)] = jnp.concatenate(
+                    pieces, axis=1
+                ).astype(BF16)
+        kept = wires.keep(gating_cut.at[place.row], gating.at[place.row])
+        moved = [
+            wires.push(gating_cut.at[other], gating.at[place.row], device)
+            for other, device in peers
         ]
-        base = wires.count
-        wires.count += 16
-        copies = []
-        for index, device in enumerate(users):
-            copy = pltpu.make_async_remote_copy(
-                src_ref=merge_own,
-                dst_ref=target,
-                send_sem=wires.send.at[base + index],
-                recv_sem=wires.recv.at[base + place.row * 4 + place.z],
-                device_id=device,
-                device_id_type=MESH,
-            )
-            here = pltpu.make_async_copy(
-                merge_own, target, wires.recv.at[base + place.row * 4 + place.z]
-            )
-            alone = (device["dp"] == place.dp) & same
-            copies.append((copy, alone))
-
-            @pl.when(alone)
-            def _():
-                here.start()
-
-            @pl.when(jnp.logical_not(alone))
-            def _():
-                copy.start()
-
-        yield 28.0
-        for index in range(16):
-            pltpu.make_async_copy(merge_own, target, wires.recv.at[base + index]).wait()
-        for copy, alone in copies:
-
-            @pl.when(jnp.logical_not(alone))
-            def _():
-                copy.wait_send()
+        yield 40.0
+        kept.wait()
+        for copy in moved:
+            copy.wait_recv()
 
     interleave(
+        line_gather(place, wires, input_own, inputs, tile_block, tile_half, 0.1, 11.4),
         exchange(),
-        merge_rows(),
-        line_gather(place, wires, input_own, inputs, tile_block, tile_half, 0.1, 11.4),
+        gating_exchange(),
+        line_gather(place, wires, back_own, back, tile_block, tile_half, 6.0, 22.0),
     )
     wires.drain()
 
 
 def middle_kernel(
-    part, input_rows, gains, gating_own, down_own, back_own,
-    middle, normed, gating, down, back,
+    part, input_rows, gains, gating_own,
+    middle, normed, gating,
     *scratch,
 ):
     line_scratch, (normed_own, send, recv, local) = scratch[:4], scratch[4:]
@@ -612,39 +650,23 @@
         kept = [
             wires.keep(gating_own.at[r], gating.at[r, place.dp]) for r in range(4)
         ]
-        rows = pl.ds(pl.multiple_of(place.dp * PIECE, PIECE), PIECE)
-        kept.append(wires.keep(down_own, down.at[rows]))
         for copy in kept:
             copy.wait()
-        plans = [
+        yield from nested(
             ring_gather(place, wires, Rows(2 * HIDDEN), gating, side, 0.5, 4.3) for side in (0, 1)
-        ] + [ring_gather(place, wires, Flat(), down, side, 0.6, 4.3) for side in (0, 1)]
-        pending = [(next(plan), order, plan) for order, plan in enumerate(plans)]
-        while pending:
-            pending.sort(key=lambda entry: entry[:2])
-            when, order, plan = pending[0]
-            yield when
-            try:
-                pending[0] = (max(when, next(plan)), order, plan)
-            except StopIteration:
-                pending.pop(0)
-
-    interleave(
-        main(),
-        weights(),
-        line_gather(place, wires, back_own, back, tile_block, tile_half, 25.5, 22.0),
-    )
+        )
+
+    interleave(main(), weights())
     wires.drain()
 
 
 def branch_kernel(
-    part, middle, back_rows, gains, gating_part, down_part,
-    grad_middle, branch, gain_part, gating_sum, down_sum,
+    part, middle, back_rows, gains, gating_part,
+    grad_middle, branch, gain_part, gating_sum,
     *scratch,
 ):
     line_scratch, scratch = scratch[:4], scratch[4:]
     gating_scratch, scratch = scratch[:14], scratch[14:]
-    down_scratch, scratch = scratch[:14], scratch[14:]
     branch_own, send, recv, local = scratch
     place = Place()
     wires = Wires(send, recv, local)
@@ -671,7 +693,6 @@
         )
 
     rows = Rows(2 * HIDDEN)
-    flat = Flat()
     interleave(
         main(),
         *[
@@ -681,13 +702,6 @@
             )
             for side in (0, 1)
         ],
-        *[
-            ring_scatter(
-                place, wires, flat, down_part, side, down_scratch,
-                down_sum.at[:, pl.ds(side * 1024, 1024)], 0.6, 4.3,
-            )
-            for side in (0, 1)
-        ],
     )
     wires.drain()
 
@@ -702,31 +716,26 @@
 
 def finish_kernel(
     part, down_out, middle, grad_middle, input_rows, gains, gain_part,
-    heads_part, merge_part, gating_sum, down_sum,
+    heads_part, merge_part, gating_sum, down_part,
     output, input_grad, gains_grad, heads_pieces, merge_pieces, gating_pieces, down_pieces,
     *scratch,
 ):
     line_scratch, scratch = scratch[:4], scratch[4:]
     out_scratch, scratch = scratch[:4], scratch[4:]
     heads_scratch, scratch = scratch[:14], scratch[14:]
+    down_scratch, scratch = scratch[:14], scratch[14:]
     (
-        heads_sum, output_own, input_grad_own, gain_rows, gain_came, gain_all, send, recv, local,
+        heads_all, heads_sum, down_sum, output_own, input_grad_own, gain_rows, gain_came, gain_all,
+        send, recv, local,
     ) = scratch
     place = Place()
     wires = Wires(send, recv, local)
-    homes, users = merge_devices(place)
+    users, homes = merge_devices(place)
     peers = [place.peer(step) for step in (1, 2, 3)]
     same = place.row == place.y
     barrier = pltpu.get_barrier_semaphore()
     devices = ring_neighbours(place) + line_neighbours(place) + [p for _, p in peers]
-    for device in devices:
-        pl.semaphore_signal(barrier, inc=1, device_id=device, device_id_type=MESH)
-    for device in users:
-        alone = (device["dp"] == place.dp) & same
-
-        @pl.when(jnp.logical_not(alone))
-        def _():
-            pl.semaphore_signal(barrier, inc=1, device_id=device, device_id_type=MESH)
+    signal_others(place, devices + users)
 
     def far(step):
         index = lax.rem(place.col * 16 + place.dp + step, 32)
@@ -737,10 +746,7 @@
         return carry
 
     lax.fori_loop(1, 32, greet, 0)
-    pl.semaphore_wait(barrier, len(devices) + 31 + 16 - same.astype(jnp.int32))
-
-    def column_block(ref, row):
-        return ref.at[:, pl.ds(pl.multiple_of(row * 512, 512), 512)]
+    pl.semaphore_wait(barrier, len(devices) + 31 + 4 - same.astype(jnp.int32))
 
     def own_rows(ref, row):
         return ref.at[pl.ds(pl.multiple_of(row * OWN, OWN), OWN)]
@@ -840,97 +846,227 @@
         for copy in moved:
             copy.wait_recv()
 
-    def heads():
+    def weights():
+        yield 0.1
+        for row in range(4):
+            for slot in range(16):
+                rows = pl.ds((row * 16 + slot) * 32, 32)
+                heads_all[row, slot, :, pl.ds(0, HEADS_COLS)] = heads_part[rows, :]
+                y, z = divmod(slot, 4)
+                for half in range(2):
+                    piece = merge_part[
+                        pl.ds(z * 64 + y * 16, 16), pl.ds(row * 512 + half * 256, 256)
+                    ]
+                    heads_all[row, slot, pl.ds(16 * half, 16), pl.ds(HEADS_COLS, 256)] = piece
         plans = [
             ring_scatter(
-                place, wires, Rows(HEADS_COLS), heads_part, side, heads_scratch,
-                heads_sum.at[pl.ds(2 * side, 2)], 0.2, 1.1,
+                place, wires, Rows(HEADS_COLS + 256), heads_all, side, heads_scratch,
+                heads_sum.at[pl.ds(2 * side, 2)], 0.2, 1.8,
+            )
+            for side in (0, 1)
+        ] + [
+            ring_scatter(
+                place, wires, Flat(), down_part, side, down_scratch,
+                down_sum.at[:, pl.ds(side * 1024, 1024)], 0.3, 4.0,
             )
             for side in (0, 1)
         ]
-        pending = [(next(plan), order, plan) for order, plan in enumerate(plans)]
-        while pending:
-            pending.sort(key=lambda entry: entry[:2])
-            when, order, plan = pending[0]
-            yield when
-            try:
-                pending[0] = (max(when, next(plan)), order, plan)
-            except StopIteration:
-                pending.pop(0)
-        yield 18.0
-        yield from back_pieces(lambda row: heads_sum.at[row], heads_pieces, 40.0)
+        yield from nested(plans)
+        merge_wait = merge_exchange(
+            place, wires, homes,
+            lambda row: heads_sum.at[row, :, pl.ds(HEADS_COLS, 256)],
+            lambda row: merge_pieces.at[place.y],
+            place.y,
+        )
+        heads_back = back_pieces(
+            lambda row: heads_sum.at[row, :, pl.ds(0, HEADS_COLS)], heads_pieces, 50.0
+        )
+        next(heads_back)
+        down_back = back_pieces(lambda row: column_block(down_sum, row), down_pieces, 50.0)
+        next(down_back)
+        yield 50.0
+        for _ in heads_back:
+            pass
+        for _ in down_back:
+            pass
+        merge_wait()
 
     def gating():
         yield 0.4
         yield from back_pieces(lambda row: gating_sum.at[row], gating_pieces, 41.0)
 
-    def down():
-        yield 0.5
-        yield from back_pieces(lambda row: column_block(down_sum, row), down_pieces, 41.0)
-
-    def merge():
-        yield 0.1
-        base = wires.count
-        wires.count += 32
-        copies = []
-        for index, device in enumerate(homes):
-            z, row = index // 4, index % 4
-            source = merge_part.at[pl.ds(z * 64, 64), pl.ds(row * 512, 512)]
-            copy = pltpu.make_async_remote_copy(
-                src_ref=source,
-                dst_ref=merge_pieces.at[place.dp],
-                send_sem=wires.send.at[base + index],
-                recv_sem=wires.recv.at[base + 16 + place.dp],
-                device_id=device,
-                device_id_type=MESH,
+    interleave(gradient(), outputs(), weights(), gating())
+    wires.drain()
+
+
+def turn(tile, cosine, sine):
+    lane = lax.broadcasted_iota(jnp.int32, tile.shape, 1)
+    first = lax.rem(lane, HEAD_SIZE) < HEAD_SIZE // 2
+    swapped = jnp.where(first, pltpu.roll(tile, 96, axis=1), pltpu.roll(tile, 32, axis=1))
+    return tile * cosine + swapped * sine
+
+
+def keys_only(cosine, sine):
+    key = lax.broadcasted_iota(jnp.int32, cosine.shape, 1) < HEAD_SIZE
+    return jnp.where(key, cosine, 1.0), jnp.where(key, sine, 0.0)
+
+
+def heads_weight_of(heads):
+    return heads[:, :, :, pl.ds(0, HEADS_COLS)].reshape(MODEL_WIDTH, HEADS_COLS)
+
+
+QUERY_BLOCK = 256
+
+
+def forward_kernel(
+    inputs, gains, heads, cosine, sine,
+    normed, query, pair, sums, attended, merge, part,
+):
+    for row in range(4):
+        for slot in range(16):
+            y, z = divmod(slot, 4)
+            for half in range(2):
+                merge[pl.ds(z * 64 + y * 16, 16), pl.ds(row * 512 + half * 256, 256)] = heads[
+                    row, slot, pl.ds(16 * half, 16), pl.ds(HEADS_COLS, 256)
+                ]
+
+    def project(index, carry):
+        at = pl.ds(pl.multiple_of(index * 128, 128), 128)
+        wide = inputs[at, :].astype(F32)
+        scale = lax.rsqrt(jnp.sum(wide * wide, axis=1, keepdims=True) / MODEL_WIDTH + EPS_NORM)
+        low = (wide * scale * gains[0:1, :]).astype(BF16)
+        normed[at, :] = low
+        mixed = product(low, heads_weight_of(heads))
+        cos, sin = cosine[at, :], sine[at, :]
+        query[at, pl.ds(0, 128)] = turn(mixed[:, :128], cos, sin).astype(BF16)
+        query[at, pl.ds(128, 128)] = turn(mixed[:, 128:256], cos, sin).astype(BF16)
+        pair[at, :] = turn(mixed[:, 256:], *keys_only(cos, sin)).astype(BF16)
+        return carry
+
+    lax.fori_loop(0, SEQ // 128, project, 0)
+    scale = HEAD_SIZE ** (-0.5)
+    rows_at = lax.broadcasted_iota(jnp.int32, (QUERY_BLOCK, QUERY_BLOCK), 0)
+    keys_at = lax.broadcasted_iota(jnp.int32, (QUERY_BLOCK, QUERY_BLOCK), 1)
+    for block in range(SEQ // QUERY_BLOCK):
+        at = pl.ds(block * QUERY_BLOCK, QUERY_BLOCK)
+        before = block * QUERY_BLOCK
+        out = []
+        for head in range(4):
+            rows = query[at, pl.ds(head * HEAD_SIZE, HEAD_SIZE)]
+            scores = [
+                jnp.where(
+                    rows_at >= keys_at,
+                    contract_last(rows, pair[at, pl.ds(0, HEAD_SIZE)]) * scale,
+                    MASK_FILL,
+                )
+            ]
+            if before:
+                scores.append(
+                    contract_last(rows, pair[pl.ds(0, before), pl.ds(0, HEAD_SIZE)]) * scale
+                )
+            top = functools.reduce(
+                jnp.maximum, [jnp.max(part_, axis=1, keepdims=True) for part_ in scores]
             )
-            here = pltpu.make_async_copy(
-                source, merge_pieces.at[place.dp], wires.recv.at[base + 16 + place.dp]
+            powers = [jnp.exp(part_ - top) for part_ in scores]
+            total = functools.reduce(
+                lambda a, b: a + b, [jnp.sum(part_, axis=1, keepdims=True) for part_ in powers]
             )
-            alone = (device["dp"] == place.dp) & (device["row"] == place.row)
-            copies.append((copy, alone))
-
-            @pl.when(alone)
-            def _():
-                here.start()
-
-            @pl.when(jnp.logical_not(alone))
-            def _():
-                copy.start()
-
-        yield 42.0
-        for index in range(16):
-            pltpu.make_async_copy(
-                merge_part.at[pl.ds(0, 64), pl.ds(0, 512)],
-                merge_pieces.at[index],
-                wires.recv.at[base + 16 + index],
-            ).wait()
-        for copy, alone in copies:
-
-            @pl.when(jnp.logical_not(alone))
-            def _():
-                copy.wait_send()
-
-    interleave(gradient(), outputs(), heads(), gating(), down(), merge())
-    wires.drain()
-
-
-def rope_tables(positions):
+            low = [(part_ * (1.0 / total)).astype(BF16) for part_ in powers]
+            result = product(low[0], pair[at, pl.ds(HEAD_SIZE, HEAD_SIZE)])
+            if before:
+                result += product(low[1], pair[pl.ds(0, before), pl.ds(HEAD_SIZE, HEAD_SIZE)])
+            sums[at, pl.ds(head, 1)] = top + jnp.log(total)
+            out.append(result.astype(BF16))
+        attended[at, :] = jnp.concatenate(out, axis=1)
+
+    def merge_rows(index, carry):
+        at = pl.ds(pl.multiple_of(index * 128, 128), 128)
+        part[at, :] = product(attended[at, :], merge[...]).astype(BF16)
+        return carry
+
+    lax.fori_loop(0, SEQ // 128, merge_rows, 0)
+
+
+def backward_kernel(
+    branch, merge, heads, query, pair, sums, cosine, sine,
+    grad_mixed, part,
+    grad_attended, grad_key, grad_value, key_columns,
+):
+    def attended_rows(index, carry):
+        at = pl.ds(pl.multiple_of(index * 128, 128), 128)
+        grad_attended[at, :] = contract_last(branch[at, :], merge[...]).astype(BF16)
+        return carry
+
+    lax.fori_loop(0, SEQ // 128, attended_rows, 0)
+    key_columns[...] = jnp.transpose(pair[...].astype(F32))[:HEAD_SIZE].astype(BF16)
+    grad_key[...] = jnp.zeros_like(grad_key)
+    grad_value[...] = jnp.zeros_like(grad_value)
+    scale = HEAD_SIZE ** (-0.5)
+    keys_at = lax.broadcasted_iota(jnp.int32, (QUERY_BLOCK, QUERY_BLOCK), 0)
+    rows_at = lax.broadcasted_iota(jnp.int32, (QUERY_BLOCK, QUERY_BLOCK), 1)
+    for block in range(SEQ // QUERY_BLOCK):
+        at = pl.ds(block * QUERY_BLOCK, QUERY_BLOCK)
+        before = block * QUERY_BLOCK
+        for two in range(2):
+            turned = []
+            for head in (2 * two, 2 * two + 1):
+                columns = pl.ds(head * HEAD_SIZE, HEAD_SIZE)
+                rows, back = query[at, columns], grad_attended[at, columns]
+                log_total = sums[pl.ds(head, 1), at]
+                spans = [at] + ([pl.ds(0, before)] if before else [])
+                softs, grads = [], []
+                for span in spans:
+                    scores = contract_last(pair[span, pl.ds(0, HEAD_SIZE)], rows) * scale
+                    soft = jnp.exp(scores - log_total)
+                    if span is at:
+                        soft = jnp.where(rows_at >= keys_at, soft, 0.0)
+                    softs.append(soft)
+                    grads.append(contract_last(pair[span, pl.ds(HEAD_SIZE, HEAD_SIZE)], back))
+                inner = functools.reduce(
+                    lambda a, b: a + b,
+                    [jnp.sum(s * g, axis=0, keepdims=True) for s, g in zip(softs, grads)],
+                )
+                result = 0.0
+                for span, soft, grad in zip(spans, softs, grads):
+                    low = (soft * (grad - inner)).astype(BF16)
+                    grad_key[span, :] += product(low, rows)
+                    grad_value[span, :] += product(soft.astype(BF16), back)
+                    result += product(key_columns[:, span], low)
+                turned.append(result)
+            tile = jnp.transpose(jnp.concatenate(turned, axis=0)) * scale
+            grad_mixed[at, pl.ds(two * 128, 128)] = turn(
+                tile, cosine[at, :], -sine[at, :]
+            ).astype(BF16)
+
+    def finish_rows(index, carry):
+        at = pl.ds(pl.multiple_of(index * 128, 128), 128)
+        cos, sin = keys_only(cosine[at, :], sine[at, :])
+        tile = jnp.concatenate([grad_key[at, :] * scale, grad_value[at, :]], axis=1)
+        grad_mixed[at, pl.ds(256, 128)] = turn(tile, cos, -sin).astype(BF16)
+        part[at, :] = contract_last(grad_mixed[at, :], heads_weight_of(heads)).astype(BF16)
+        return carry
+
+    lax.fori_loop(0, SEQ // 128, finish_rows, 0)
+
+
+def local_call(kernel, outs, ins, scratch, flops):
+    return pl.pallas_call(
+        kernel,
+        out_shape=outs,
+        in_specs=[pl.BlockSpec(memory_space=pltpu.VMEM)] * len(ins),
+        out_specs=[pl.BlockSpec(memory_space=pltpu.VMEM)] * len(outs),
+        scratch_shapes=scratch,
+        compiler_params=pltpu.CompilerParams(vmem_limit_bytes=VMEM_BYTES),
+        cost_estimate=pl.CostEstimate(flops=flops, bytes_accessed=2**24, transcendentals=2**22),
+    )(*ins)
+
+
+def rope_tables():
     half_width = HEAD_SIZE // 2
-    frequency = ROPE_BASE ** (-jnp.arange(half_width, dtype=jnp.float32) * 2.0 / HEAD_SIZE)
-    angles = positions.astype(jnp.float32)[:, None] * frequency[None, :]
-    return (jnp.cos(angles), jnp.sin(angles))
-
-
-def rotate(vector, cosine_rows, sine_rows):
-    piece_one, piece_two = jnp.split(vector, 2, axis=-1)
-    return jnp.concatenate(
-        [
-            piece_one * cosine_rows - piece_two * sine_rows,
-            piece_two * cosine_rows + piece_one * sine_rows,
-        ],
-        axis=-1,
-    )
+    frequency = ROPE_BASE ** (-jnp.arange(half_width, dtype=F32) * 2.0 / HEAD_SIZE)
+    angles = jnp.arange(SEQ, dtype=F32)[:, None] * frequency[None, :]
+    cosine, sine = jnp.cos(angles), jnp.sin(angles)
+    return jnp.tile(cosine, (1, 4)), jnp.concatenate([-sine, sine, -sine, sine], axis=1)
 
 
 def product(left, right):
@@ -956,14 +1092,6 @@
     return (updated, mean_new, square_new)
 
 
-def pack_heads(weight):
-    groups = weight.astype(BF16).reshape(32, 2, 640)
-    query = groups[:, :, :512].reshape(32, 2, 2, 256).transpose(1, 2, 0, 3)
-    pair = groups[:, :, 512:].transpose(1, 0, 2)[:, None]
-    pair = jnp.broadcast_to(pair, (2, 2, 32, 128))
-    return jnp.concatenate([query, pair], axis=3).reshape(4, 32, HEADS_COLS)
-
-
 def unpack_heads(pieces):
     pieces = pieces.astype(F32).reshape(2, 2, 32, HEADS_COLS)
     query = pieces[..., :256].transpose(2, 0, 1, 3).reshape(32, 2, 512)
@@ -971,20 +1099,13 @@
     return jnp.concatenate([query, pair], axis=2).reshape(32, 1280)
 
 
-def pack_gating(weight):
-    cut = weight.astype(BF16).reshape(32, 2, 16, 4, PIECE_USED).transpose(3, 0, 1, 2, 4)
-    cut = jnp.pad(cut, ((0, 0),) * 4 + ((0, PIECE - PIECE_USED),))
-    return cut.reshape(4, 32, 2 * HIDDEN)
-
-
 def unpack_gating(pieces):
     cut = pieces.reshape(4, 32, 2, 16, PIECE)[..., :PIECE_USED]
     return cut.transpose(1, 2, 3, 0, 4).reshape(32, 2, 2816).astype(F32)
 
 
-def pack_down(weight):
-    cut = weight.astype(BF16).reshape(4, PIECE_USED, 512)
-    return jnp.pad(cut, ((0, 0), (0, PIECE - PIECE_USED), (0, 0)))
+def unpack_merge(pieces):
+    return pieces.reshape(4, 2, 16, 256).transpose(0, 2, 1, 3).reshape(64, 512).astype(F32)
 
 
 def unpack_down(pieces):
@@ -1011,85 +1132,75 @@
     down_second,
 ):
     ANY, VMEM = pl.ANY, pltpu.VMEM
-    head_scale = HEAD_SIZE ** (-0.5)
     row, col = lax.axis_index("row"), lax.axis_index("col")
     line = col * 4 + row
 
     def own_rows(values):
         return lax.dynamic_slice_in_dim(values, line * OWN, OWN, axis=0)
 
-    w_heads, gating_own, down_own, w_merge, inputs, gains = call(
+    w_heads, gating_own, w_down, inputs, back, gains = call(
         start_kernel,
         [
-            (shape(4, 16, 32, HEADS_COLS), ANY),
-            (shape(4, 32, 2 * HIDDEN), ANY),
-            (shape(PIECE, MODEL_WIDTH), ANY),
-            (shape(256, MODEL_WIDTH), ANY),
-            (shape(SEQ, MODEL_WIDTH), ANY),
-            (shape(4, 8, 128, dtype=F32), ANY),
+            (shape(4, 16, 32, HEADS_COLS + 256), VMEM),
+            (shape(4, 32, 2 * HIDDEN), VMEM),
+            (shape(16 * PIECE, MODEL_WIDTH), VMEM),
+            (shape(SEQ, MODEL_WIDTH), VMEM),
+            (shape(SEQ, MODEL_WIDTH), VMEM),
+            (shape(4, 8, 128, dtype=F32), VMEM),
         ],
         [
-            (pack_heads(heads_projection_weight), ANY),
-            (pack_gating(gating_weight), ANY),
-            (pack_down(down_weight), ANY),
-            (merge_weight.astype(BF16), ANY),
-            (block_input, ANY),
-            (norm_gains.reshape(8, 128), ANY),
+            (heads_projection_weight, VMEM),
+            (merge_weight, VMEM),
+            (gating_weight, VMEM),
+            (down_weight, VMEM),
+            (block_input, VMEM),
+            (cotangent, VMEM),
+            (norm_gains.reshape(8, 128), VMEM),
         ],
-        [],
-        100,
+        [
+            pltpu.VMEM((4, 32, HEADS_COLS), BF16),
+            pltpu.VMEM((4, 32, 256), BF16),
+            pltpu.VMEM((4, 32, 2 * HIDDEN), BF16),
+            pltpu.VMEM((4, PIECE, 512), BF16),
+        ],
+        140,
         0,
         2**24,
     )
-    w_heads = w_heads.reshape(MODEL_WIDTH, HEADS_COLS)
     gains = gains.reshape(4, 2, 512).transpose(1, 0, 2).reshape(2, MODEL_WIDTH)
     input_rows = own_rows(inputs)
-    wide = inputs.astype(F32)
-    scale_one = lax.rsqrt(jnp.mean(wide * wide, axis=1, keepdims=True) + EPS_NORM)
-    normed_one = (wide * scale_one * gains[0]).astype(BF16)
-
-    mixed = product(normed_one, w_heads)
-    cosine_rows, sine_rows = rope_tables(jnp.arange(SEQ, dtype=jnp.int32))
-    query = rotate(
-        mixed[:, :256].reshape(SEQ, 4, HEAD_SIZE), cosine_rows[:, None], sine_rows[:, None]
-    ).astype(BF16)
-    key = rotate(mixed[:, 256:320], cosine_rows, sine_rows).astype(BF16)
-    value = mixed[:, 320:].astype(BF16)
-    causal = jnp.arange(SEQ)[:, None] >= jnp.arange(SEQ)[None, :]
-
-    def scores_of():
-        raw = jnp.einsum("tqd,sd->qts", query, key, preferred_element_type=F32) * head_scale
-        return jnp.where(causal, raw, MASK_FILL)
-
-    scores = scores_of()
-    row_max = jnp.max(scores, axis=-1, keepdims=True)
-    exponent = jnp.exp(scores - row_max)
-    exp_total = jnp.sum(exponent, axis=-1, keepdims=True)
-    probs_low = (exponent / exp_total).astype(BF16)
-    log_total = row_max + jnp.log(exp_total)
-    attended = jnp.einsum("qts,sd->tqd", probs_low, value, preferred_element_type=F32)
-    attended = attended.reshape(SEQ, 256).astype(BF16)
-    merged = product(attended, w_merge).astype(BF16)
-
-    middle, normed_two, w_gating, w_down, back = call(
+    cosine, sine = rope_tables()
+    normed_one, query, pair, sums, attended, w_merge, merged = local_call(
+        forward_kernel,
+        [
+            shape(SEQ, MODEL_WIDTH),
+            shape(SEQ, 256),
+            shape(SEQ, 128),
+            shape(SEQ, 128, dtype=F32),
+            shape(SEQ, 256),
+            shape(256, MODEL_WIDTH),
+            shape(SEQ, MODEL_WIDTH),
+        ],
+        [inputs, gains, w_heads, cosine, sine],
+        [],
+        2**32,
+    )
+
+    middle, normed_two, w_gating = call(
         middle_kernel,
         [
             (shape(OWN, MODEL_WIDTH, dtype=F32), VMEM),
-            (shape(SEQ, MODEL_WIDTH), ANY),
-            (shape(4, 16, 32, 2 * HIDDEN), ANY),
-            (shape(16 * PIECE, MODEL_WIDTH), ANY),
-            (shape(SEQ, MODEL_WIDTH), ANY),
+            (shape(SEQ, MODEL_WIDTH), VMEM),
+            (shape(4, 16, 32, 2 * HIDDEN), VMEM),
         ],
         [
             (merged, VMEM),
             (input_rows, VMEM),
             (gains, VMEM),
-            (gating_own, ANY),
-            (down_own, ANY),
-            (cotangent, ANY),
+            (gating_own, VMEM),
         ],
         LINE_SCATTER_SCRATCH + [pltpu.VMEM((OWN, MODEL_WIDTH), BF16)],
-        130,
+        100,
         1,
         2**25,
     )
@@ -1109,14 +1220,13 @@
     gating_part = token_product(normed_two, grad_gated).astype(BF16)
     normed_two_part = contract_last(grad_gated, w_gating).astype(BF16)
 
-    grad_middle, branch, gain_part, gating_sum, down_sum = call(
+    grad_middle, branch, gain_part, gating_sum = call(
         branch_kernel,
         [
             (shape(OWN, MODEL_WIDTH, dtype=F32), VMEM),
-            (shape(SEQ, MODEL_WIDTH), ANY),
+            (shape(SEQ, MODEL_WIDTH), VMEM),
             (shape(8, MODEL_WIDTH, dtype=F32), VMEM),
             (shape(4, 32, 2 * HIDDEN), VMEM),
-            (shape(PIECE, MODEL_WIDTH), VMEM),
         ],
         [
             (normed_two_part, VMEM),
@@ -1124,37 +1234,29 @@
             (own_rows(back), VMEM),
             (gains, VMEM),
             (gating_part.reshape(4, 16, 32, 2 * HIDDEN), VMEM),
-            (down_part, VMEM),
         ],
         LINE_SCATTER_SCRATCH
         + ring_scatter_scratch(Rows(2 * HIDDEN))
-        + ring_scatter_scratch(Flat())
         + [pltpu.VMEM((OWN, MODEL_WIDTH), BF16)],
-        130,
+        100,
         2,
         2**25,
     )
 
     merge_part = token_product(attended, branch).astype(BF16)
-    grad_attended = contract_last(branch, w_merge).astype(BF16).reshape(SEQ, 4, HEAD_SIZE)
-    soft = jnp.exp(scores_of() - log_total)
-    grad_probs = jnp.einsum("tqd,sd->qts", grad_attended, value, preferred_element_type=F32)
-    inner_sum = jnp.sum(soft * grad_probs, axis=-1, keepdims=True)
-    grad_scores = (soft * (grad_probs - inner_sum)).astype(BF16)
-    grad_query = (
-        jnp.einsum("qts,sd->tqd", grad_scores, key, preferred_element_type=F32) * head_scale
-    )
-    grad_key = (
-        jnp.einsum("qts,tqd->sd", grad_scores, query, preferred_element_type=F32) * head_scale
-    )
-    grad_value = jnp.einsum(
-        "qts,tqd->sd", soft.astype(BF16), grad_attended, preferred_element_type=F32
-    )
-    grad_query = rotate(grad_query, cosine_rows[:, None], -sine_rows[:, None]).reshape(SEQ, 256)
-    grad_key = rotate(grad_key, cosine_rows, -sine_rows)
-    grad_mixed = jnp.concatenate([grad_query, grad_key, grad_value], axis=1).astype(BF16)
+    grad_mixed, normed_one_part = local_call(
+        backward_kernel,
+        [shape(SEQ, HEADS_COLS), shape(SEQ, MODEL_WIDTH)],
+        [branch, w_merge, w_heads, query, pair, sums[:, :8].T, cosine, sine],
+        [
+            pltpu.VMEM((SEQ, 256), BF16),
+            pltpu.VMEM((SEQ, HEAD_SIZE), F32),
+            pltpu.VMEM((SEQ, HEAD_SIZE), F32),
+            pltpu.VMEM((HEAD_SIZE, SEQ), BF16),
+        ],
+        2**33,
+    )
     heads_part = token_product(normed_one, grad_mixed).astype(BF16)
-    normed_one_part = contract_last(grad_mixed, w_heads).astype(BF16)
 
     (
         block_output, input_grad, gains_grad,
@@ -1162,13 +1264,13 @@
     ) = call(
         finish_kernel,
         [
-            (shape(512, 512), ANY),
-            (shape(512, 512, dtype=F32), ANY),
+            (shape(512, 512), VMEM),
+            (shape(512, 512, dtype=F32), VMEM),
             (shape(8, 512, dtype=F32), VMEM),
-            (shape(4, 32, HEADS_COLS), ANY),
-            (shape(16, 64, 512), ANY),
-            (shape(4, 32, 2 * HIDDEN), ANY),
-            (shape(4, PIECE, 512), ANY),
+            (shape(4, 32, HEADS_COLS), VMEM),
+            (shape(4, 32, 256), VMEM),
+            (shape(4, 32, 2 * HIDDEN), VMEM),
+            (shape(4, PIECE, 512), VMEM),
         ],
         [
             (normed_one_part, VMEM),
@@ -1178,16 +1280,19 @@
             (input_rows, VMEM),
             (gains, VMEM),
             (gain_part, VMEM),
-            (heads_part.reshape(4, 16, 32, HEADS_COLS), VMEM),
-            (merge_part, ANY),
-            (gating_sum, ANY),
-            (down_sum, ANY),
+            (heads_part, VMEM),
+            (merge_part, VMEM),
+            (gating_sum, VMEM),
+            (down_part, VMEM),
         ],
         LINE_SCATTER_SCRATCH
         + LINE_SCATTER_SCRATCH
-        + ring_scatter_scratch(Rows(HEADS_COLS))
+        + ring_scatter_scratch(Rows(HEADS_COLS + 256))
+        + ring_scatter_scratch(Flat())
         + [
-            pltpu.VMEM((4, 32, HEADS_COLS), BF16),
+            pltpu.VMEM((4, 16, 32, HEADS_COLS + 256), BF16),
+            pltpu.VMEM((4, 32, HEADS_COLS + 256), BF16),
+            pltpu.VMEM((PIECE, MODEL_WIDTH), BF16),
             pltpu.VMEM((OWN, MODEL_WIDTH), BF16),
             pltpu.VMEM((OWN, MODEL_WIDTH), F32),
             pltpu.VMEM((2, 8, MODEL_WIDTH), F32),
@@ -1200,7 +1305,7 @@
     )
     gains_grad = gains_grad[:2]
     heads_grad = unpack_heads(heads_pieces)
-    merge_grad = jnp.sum(merge_pieces.astype(F32), axis=0)
+    merge_grad = unpack_merge(merge_pieces)
     gating_grad = unpack_gating(gating_pieces)
     down_grad = unpack_down(down_pieces)
     gains_next, gains_mean, gains_square = adamw(

time: 510 us -> 414 us (0.81)
  matrix products: 101 us -> 51.3 us
  other arithmetic: 40 us -> 16.9 us
  Pallas kernels: 336 us -> 320 us
  local copies, waits for them, and re-layouts: 23.2 us -> 18 us
    pallas_call x4, Pallas kernels: 336 us -> 269 us  [call(): pl.pallas_call(kernel, out_shape=[shape for shape, _ in outs], in_specs=[...]
    pallas_call x0 -> x2, Pallas kernels: none -> 51.2 us  [local_call(): pl.pallas_call(kernel, out_shape=outs, in_specs=[pl.BlockSpec(memory_spac...]
    dot_general x6 -> x0, matrix products: 35.4 us -> none  [the longest x1 8.6 us: body(): jnp.einsum('qts,tqd->sd', soft.astype(BF16), grad_attended, preferred_ele...]
    reduce_sum x3 -> x0, other arithmetic: 12.6 us -> none  [the longest x1 8 us: body(): exp_total = jnp.sum(exponent, axis=-1, keepdims=True)]
    convert_element_type x6 -> x1, other arithmetic: 12.8 us -> 0.91 us  [unpack_merge(): pieces.reshape(4, 2, 16, 256).transpose(0, 2, 1, 3).reshape(64, 512)]
    dot_general x4 -> x2, matrix products: 22.1 us -> 13.1 us  [contract_last(): lax.dot_general(left, right, (((1,), (1,)), ((), ())), preferred_element_...]
    dot_general x4 -> x2, matrix products: 22.5 us -> 15.6 us  [product(): return jnp.dot(left, right, preferred_element_type=F32)]
    reshape x7 -> x0, local copies, waits for them, and re-layouts: 6.16 us -> none  [the longest x2 3.24 us: pack_gating(): weight.astype(BF16).reshape(32, 2, 16, 4, PIECE_USED)]
where the time goes in v2:
time: 414 us; the launch traced here: 408 us
  Pallas kernels  320 us (77%)
  matrix products  51.3 us (12%)
  local copies, waits for them, and re-layouts  18 us (4%)
  other arithmetic  16.9 us (4%)
    pallas_call x4, Pallas kernels, call(): pl.pallas_call(kernel, out_shape=[shape for shape, _ in outs], in_specs=[...  269 us
    pallas_call x2, Pallas kernels, local_call(): pl.pallas_call(kernel, out_shape=outs, in_specs=[pl.BlockSpec(memory_spac...  51.2 us
    dot_general x4, matrix products, token_product(): lax.dot_general(left, right, (((0,), (0,)), ((), ())), preferred_element_...  22.6 us
    dot_general x2, matrix products, product(): return jnp.dot(left, right, preferred_element_type=F32)  15.6 us
    dot_general x2, matrix products, contract_last(): lax.dot_general(left, right, (((1,), (1,)), ((), ())), preferred_element_...  13.1 us
    sub x5, other arithmetic, adamw(): current - step_rate * (mean_hat / (jnp.sqrt(square_hat) + EPS_ADAM) + dec...  10.5 us

profile of v2, /device:TPU:25, one launch (start us, length us, event | category | flops | bytes accessed | tf_op | source)
XLA Modules:
  0.0 407.6 jit_solution(17850272060097999358)
XLA Ops:
  0.7 1.3 reshape.117.gains_own
  2.0 2.0 fusion.5
  3.9 1.3 pad_maximum_fusion.3.sine
  5.2 0.2 copy.73
  5.4 0.1 tile.13
  5.4 1.0 copy.74.cosine
  6.4 69.6 %shard_map.336 = (bf16[4,16,32,640]{3,2,1,0:T(8,128)(2,1)}, bf16[4,32,1536]{2,1,0:T(8,128)(2,1)}, bf16[768,2048]{1,0:T(8,128)(2,1)}, bf16[1024,2048]{1,0:T(8,128...) custom-call(f32[32,1280]{1,0:T(8,128)} %heads_weight.1, f32[64,512]{1,0:T(8,128)} %merge_weight.1, ...), custom_call_target="tpu_custom_call" | custom-call | bytes 16777216 | tf_op jit(solution)/shard_map/pallas_call | solution.py:428
  76.1 0.7 reshape.118
  76.8 0.6 copy.90
  77.4 2.3 constant_dynamic-slice_fusion
  79.7 25.1 %shard_map.337 = (bf16[1024,2048]{1,0:T(8,128)(2,1)}, bf16[1024,256]{1,0:T(8,128)(2,1)}, bf16[1024,128]{1,0:T(8,128)(2,1)}, f32[1024,128]{1,0:T(8,128)}, bf16[10...) custom-call(bf16[1024,2048]{1,0:T(8,128)(2,1)} %get-tuple-element.53.inputs, ...), custom_call_target="tpu_custom_call" | custom-call | flops 4294967296 | bytes 16777216 | tf_op jit(solution)/shard_map/pallas_call | solution.py:1053
  104.8 1.2 copy.77
  106.1 0.6 slice_bitcast_fusion.2.sums
  106.7 56.5 %shard_map.338 = (f32[128,2048]{1,0:T(8,128)}, bf16[1024,2048]{1,0:T(8,128)(2,1)}, bf16[4,16,32,1536]{3,2,1,0:T(8,128)(2,1)}) custom-call(bf16[1024,2048]{1,0:T(8,128)(2,1)} %get-tuple-element.56.part, bf16[128,2048]{1,0:T(8,128)(2,1)} %get-tuple-element.103.input_rows, f32[2,2048]{1,0:T(2,128)} %bitcast.68, bf16[4,32,1536]{2,1,0:T(8,128)(2,1)} %get-tuple-element.57.gating_own), custom_call_target="tpu_custom_call" | custom-call | bytes 33554432 | tf_op jit(solution)/shard_map/pallas_call | solution.py:428
  163.2 10.4 %fusion.18 = f32[1024,1536]{0,1:T(8,128)S(1)} fusion(bf16[1024,2048]{1,0:T(8,128)(2,1)} %get-tuple-element.58, bf16[2048,1536]{1,0:T(8,128)(2,1)} %bitcast.73), kind=kOutput, calls=%fused_computation.53 | convolution fusion | flops 6442450944 | bytes 16777216 | tf_op jit(solution)/shard_map/dot_general | solution.py:1073
  173.7 4.6 %multiply_convert_fusion.2 = (bf16[1024,768]{0,1:T(8,128)(2,1)S(1)}, bf16[1024,768]{0,1:T(8,128)(2,1)S(1)}, bf16[1024,768]{0,1:T(8,128)(2,1)S(1)}) fusion(f32[1024,1536]{0,1:T(8,128)S(1)} %fusion.18, bf16[1024,2048]{1,0:T(8,128)(2,1)S(1)} %copy-done.13, bf16[768,2048]{1,0:T(8,128)(2,1)S(1)} %copy-done.19), kind=kOutput, calls=%fused_computation.7 | convolution fusion | flops 3233021952 | bytes 18350080 | tf_op jit(solution)/shard_map/dot_general | solution.py:1077
  178.3 4.8 %convolution_convert_fusion.3.down_part = bf16[768,2048]{1,0:T(8,128)(2,1)} fusion(bf16[1024,768]{0,1:T(8,128)(2,1)S(1)} %get-tuple-element.98, bf16[1024,2048]{1,0:T(8,128)(2,1)S(1)} %copy-done.13), kind=kOutput, calls=%fused_computation.3 | convolution fusion | flops 3222798336 | bytes 8912896 | tf_op jit(solution)/shard_map/dot_general | solution.py:1081
  183.2 8.6 %convolution_convert_fusion.1.part = bf16[1024,2048]{1,0:T(8,128)(2,1)} fusion(bf16[2048,1536]{1,0:T(8,128)(2,1)S(1)} %bitcast.76, bf16[1024,768]{0,1:T(8,128)(2,1)S(1)} %get-tuple-element.97, bf16[1024,768]{0,1:T(8,128)(2,1)S(1)} %get-tuple-element.96), kind=kOutput, calls=%fused_computation.1 | convolution fusion | flops 6450839552 | bytes 13631488 | tf_op jit(solution)/shard_map/dot_general | solution.py:1077
  191.7 9.5 %convolution_convert_fusion = bf16[2048,1536]{1,0:T(8,128)(2,1)} fusion(bf16[1024,2048]{1,0:T(8,128)(2,1)S(1)} %copy-done.18, bf16[1024,768]{0,1:T(8,128)(2,1)S(1)} %get-tuple-element.97, bf16[1024,768]{0,1:T(8,128)(2,1)S(1)} %get-tuple-element.96), kind=kOutput, calls=%fused_computation | convolution fusion | flops 6451888128 | bytes 13631488 | tf_op jit(solution)/shard_map/dot_general | solution.py:1081
  201.2 55.5 %shard_map.339 = (f32[128,2048]{1,0:T(8,128)}, bf16[1024,2048]{1,0:T(8,128)(2,1)}, f32[8,2048]{1,0:T(8,128)}, bf16[4,32,1536]{2,1,0:T(8,128)(2,1)}) custom-call(bf16[1024,2048]{1,0:T(8,128)(2,1)} %convolution_convert_fusion.1.part, f32[128,2048]{1,0:T(8,128)} %get-tuple-element.60.middle, bf16[128,2048]{1,0:T(8,128)(2,1)} %get-tuple-element.102.back_rows, ...), custom_call_target="tpu_custom_call" | custom-call | bytes 33554432 | tf_op jit(solution)/shard_map/pallas_call | solution.py:428
  256.7 26.1 %shard_map.340 = (bf16[1024,384]{1,0:T(8,128)(2,1)}, bf16[1024,2048]{1,0:T(8,128)(2,1)}) custom-call(bf16[1024,2048]{1,0:T(8,128)(2,1)} %get-tuple-element.61.branch, bf16[256,2048]{1,0:T(8,128)(2,1)} %get-tuple-element.62.merge, bf16[4,16,32,640]{3,2,1,0:T(8,128)(2,1)} %get-tuple-element.55.heads, bf16[1024,256]{1,0:T(8,128)(2,1)} %get-tuple-element.63.query, ...), custom_call_target="tpu_custom_call" | custom-call | flops 8589934592 | bytes 16777216 | tf_op jit(solution)/shard_map/pallas_call | solution.py:1053
  282.8 6.1 %convolution_convert_fusion.4.heads_part = bf16[2048,384]{1,0:T(8,128)(2,1)} fusion(bf16[1024,2048]{1,0:T(8,128)(2,1)} %get-tuple-element.69, bf16[1024,384]{1,0:T(8,128)(2,1)} %get-tuple-element.70), kind=kOutput, calls=%fused_computation.10 | convolution fusion | flops 1611399168 | bytes 6553600 | tf_op jit(solution)/shard_map/dot_general | solution.py:1081
  288.8 2.2 convolution_convert_fusion.5.merge_part
  291.1 5.1 %convolution_convert_fusion.2.down_out = bf16[1024,2048]{1,0:T(8,128)(2,1)} fusion(bf16[1024,768]{0,1:T(8,128)(2,1)S(1)} %copy-done.22, bf16[768,2048]{1,0:T(8,128)(2,1)S(1)} %copy-done.19), kind=kOutput, calls=%fused_computation.2 | convolution fusion | flops 3223322624 | bytes 8912896 | tf_op jit(solution)/shard_map/dot_general | solution.py:1073
  296.2 87.3 %shard_map.341 = (bf16[512,512]{1,0:T(8,128)(2,1)}, f32[512,512]{1,0:T(8,128)}, f32[8,512]{1,0:T(8,128)}, bf16[4,32,384]{2,1,0:T(8,128)(2,1)}, bf16[4,32,256]{2,...) custom-call(bf16[1024,2048]{1,0:T(8,128)(2,1)} %get-tuple-element.66.part, ...), custom_call_target="tpu_custom_call" | custom-call | bytes 33554432 | tf_op jit(solution)/shard_map/pallas_call | solution.py:428
  383.5 0.0 copy-start.5
  383.6 0.0 copy-start.3
  383.7 1.5 add_subtract_fusion
  385.2 0.8 slice.39
  386.0 0.1 copy.94
  386.1 0.1 reshape.124
  386.2 0.9 convert.15
  387.2 0.0 copy-start.4
  387.2 0.9 convert_bitcast_fusion.1
  388.1 0.1 copy.83
  388.3 0.0 copy-start.6
  388.3 1.0 slice_convert_fusion
  389.3 0.8 reshape.131
  390.1 0.8 multiply_subtract_fusion.3
  390.9 0.8 multiply_subtract_fusion.2
  391.7 1.1 reshape.126
  392.8 0.3 convert_bitcast_fusion
  393.1 1.8 copy.84
  394.9 3.3 reshape.130
  398.2 2.7 multiply_subtract_fusion.1
  400.9 4.7 %multiply_subtract_fusion = (f32[32,2,2816]{2,1,0:T(2,128)}, f32[32,2,2816]{2,1,0:T(2,128)}, f32[32,2,2816]{2,1,0:T(2,128)}) fusion(f32[32,2,2816]{2,1,0:T(2,128)S(1)} %copy-done, f32[32,2,2816]{2,1,0:T(2,128)S(1)} %reshape.130, f32[32,2,2816]{2,1,0:T(2,128)} %param.29, f32[32,2,2816]{2,1,0:T(2,128)} %param.30), kind=kLoop, calls=%fused_computation.15 | loop fusion | flops 2703360 | bytes 5046272 | tf_op jit(solution)/shard_map/sub | solution.py:1089
  405.6 0.8 copy.98
  406.4 1.0 copy.99
  (53 shorter events, 0.2 us)
Async XLA Ops:
  163.2 10.5 %copy-start.13 = (bf16[1024,2048]{1,0:T(8,128)(2,1)S(1)}, bf16[1024,2048]{1,0:T(8,128)(2,1)}, u32[]{:S(2)}) copy-start(bf16[1024,2048]{1,0:T(8,128)(2,1)} %get-tuple-element.51) | copy-start | bytes 12582916
  163.2 10.5 %copy-start.19 = (bf16[768,2048]{1,0:T(8,128)(2,1)S(1)}, bf16[768,2048]{1,0:T(8,128)(2,1)}, u32[]{:S(2)}) copy-start(bf16[768,2048]{1,0:T(8,128)(2,1)} %get-tuple-element.52) | copy-start | bytes 9437188
  163.2 19.9 %slice-start = ((s8[6291456]{0:T(1024)(128)(4,1)}), s8[4194304]{0:T(1024)(128)(4,1)S(1)}, s32[]{:S(2)}) async-start(s8[6291456]{0:T(1024)(128)(4,1)} %bitcast.74), calls=%async_computation | async-start | bytes 8388608
  173.7 9.4 %slice-start.1 = ((s8[6291456]{0:T(1024)(128)(4,1)}), s8[2097152]{0:T(1024)(128)(4,1)S(1)}, s32[]{:S(2)}) async-start(s8[6291456]{0:T(1024)(128)(4,1)} %bitcast.74), calls=%async_computation.1 | async-start | bytes 4194304
  178.3 4.8 %copy-start.21 = (bf16[1024,768]{0,1:T(8,128)(2,1)}, bf16[1024,768]{0,1:T(8,128)(2,1)S(1)}, u32[]{:S(2)}) copy-start(bf16[1024,768]{0,1:T(8,128)(2,1)S(1)} %get-tuple-element.98) | copy-start | bytes 4718596
  183.2 8.6 %copy-start.18 = (bf16[1024,2048]{1,0:T(8,128)(2,1)S(1)}, bf16[1024,2048]{1,0:T(8,128)(2,1)}, u32[]{:S(2)}) copy-start(bf16[1024,2048]{1,0:T(8,128)(2,1)} %get-tuple-element.58) | copy-start | bytes 12582916
  282.8 6.1 %copy-start.17 = (bf16[1024,2048]{1,0:T(8,128)(2,1)S(1)}, bf16[1024,2048]{1,0:T(8,128)(2,1)}, u32[]{:S(2)}) copy-start(bf16[1024,2048]{1,0:T(8,128)(2,1)} %get-tuple-element.61.branch) | copy-start | bytes 12582916
  282.8 6.1 %copy-start.20 = (bf16[1024,256]{1,0:T(8,128)(2,1)S(1)}, bf16[1024,256]{1,0:T(8,128)(2,1)}, u32[]{:S(2)}) copy-start(bf16[1024,256]{1,0:T(8,128)(2,1)} %get-tuple-element.71) | copy-start | bytes 1572868
  288.8 2.3 copy-start.22
  296.2 87.4 %copy-start.14 = (f32[2,512]{1,0:T(2,128)S(1)}, f32[2,512]{1,0:T(2,128)}, u32[]{:S(2)}) copy-start(f32[2,512]{1,0:T(2,128)} %param.19) | copy-start | bytes 12292
  296.2 87.4 %copy-start.15 = (f32[2,512]{1,0:T(2,128)S(1)}, f32[2,512]{1,0:T(2,128)}, u32[]{:S(2)}) copy-start(f32[2,512]{1,0:T(2,128)} %param.20) | copy-start | bytes 12292
  296.2 87.5 %copy-start.16 = (f32[2,512]{1,0:T(2,128)S(1)}, f32[2,512]{1,0:T(2,128)}, u32[]{:S(2)}) copy-start(f32[2,512]{1,0:T(2,128)} %param.21) | copy-start | bytes 12292
  383.5 6.5 %copy-start.5 = (f32[64,512]{1,0:T(8,128)S(1)}, f32[64,512]{1,0:T(8,128)}, u32[]{:S(2)}) copy-start(f32[64,512]{1,0:T(8,128)} %merge_weight.1) | copy-start | bytes 393220
  383.6 6.5 %copy-start.11 = (f32[64,512]{1,0:T(8,128)S(1)}, f32[64,512]{1,0:T(8,128)}, u32[]{:S(2)}) copy-start(f32[64,512]{1,0:T(8,128)} %param.26) | copy-start | bytes 393220
  383.6 6.5 %copy-start.12 = (f32[64,512]{1,0:T(8,128)S(1)}, f32[64,512]{1,0:T(8,128)}, u32[]{:S(2)}) copy-start(f32[64,512]{1,0:T(8,128)} %param.27) | copy-start | bytes 393220
  383.6 7.3 %copy-start.3 = (f32[32,1280]{1,0:T(8,128)S(1)}, f32[32,1280]{1,0:T(8,128)}, u32[]{:S(2)}) copy-start(f32[32,1280]{1,0:T(8,128)} %heads_weight.1) | copy-start | bytes 491524
  383.6 7.3 %copy-start.9 = (f32[32,1280]{1,0:T(8,128)S(1)}, f32[32,1280]{1,0:T(8,128)}, u32[]{:S(2)}) copy-start(f32[32,1280]{1,0:T(8,128)} %param.23) | copy-start | bytes 491524
  383.6 7.3 %copy-start.10 = (f32[32,1280]{1,0:T(8,128)S(1)}, f32[32,1280]{1,0:T(8,128)}, u32[]{:S(2)}) copy-start(f32[32,1280]{1,0:T(8,128)} %param.24) | copy-start | bytes 491524
  383.6 8.1 %copy-start.8 = (bf16[4,32,1536]{2,1,0:T(8,128)(2,1)S(1)}, bf16[4,32,1536]{2,1,0:T(8,128)(2,1)}, u32[]{:S(2)}) copy-start(bf16[4,32,1536]{2,1,0:T(8,128)(2,1)} %get-tuple-element.78) | copy-start | bytes 1179652
  387.2 4.5 %copy-start.4 = (f32[2,4,8,640]{3,2,0,1:T(8,128)}, f32[2,4,8,640]{3,2,0,1:T(8,128)S(1)}, u32[]{:S(2)}) copy-start(f32[2,4,8,640]{3,2,0,1:T(8,128)S(1)} %copy.89) | copy-start | bytes 491524
  388.3 3.5 copy-start.6
  394.9 6.0 %copy-start = (f32[32,2,2816]{2,1,0:T(2,128)S(1)}, f32[32,2,2816]{2,1,0:T(2,128)}, u32[]{:S(2)}) copy-start(f32[32,2,2816]{2,1,0:T(2,128)} %gating_weight.1) | copy-start | bytes 2162692
  398.2 7.4 %copy-start.1 = (f32[32,2,2816]{2,1,0:T(2,128)}, f32[32,2,2816]{2,1,0:T(2,128)S(1)}, u32[]{:S(2)}) copy-start(f32[32,2,2816]{2,1,0:T(2,128)S(1)} %reshape.130) | copy-start | bytes 2162692
  400.9 4.7 %copy-start.7 = (bf16[512,512]{1,0:T(8,128)(2,1)S(1)}, bf16[512,512]{1,0:T(8,128)(2,1)}, u32[]{:S(2)}) copy-start(bf16[512,512]{1,0:T(8,128)(2,1)} %get-tuple-element.126) | copy-start | bytes 1572868
  400.9 5.5 %copy-start.2 = (f32[512,512]{1,0:T(8,128)S(1)}, f32[512,512]{1,0:T(8,128)}, u32[]{:S(2)}) copy-start(f32[512,512]{1,0:T(8,128)} %get-tuple-element.127) | copy-start | bytes 3145732
